TPU v7x, 32 devices: a whole 2x2x4 slice. The times are simulated.
32 devices in a mesh: groups: 2 (over y), fsdp: 16 (over z, x, core).
Axes of the slice: x: 2, y: 2, z: 4, core: 2. Of those that a mesh axis runs over, the one named last changes fastest.
Arguments:
- tokens: bfloat16 [4096, 8192], P(('groups', 'fsdp')), parts along dimension 0, may hold values from -6 to 6
- grad_out: bfloat16 [4096, 1024], P(('groups', 'fsdp')), parts along dimension 0, may hold values from -6 to 6
- base_weight: bfloat16 [8192, 1024], P('fsdp'), may hold values from -0.0625 to 0.0625
- shrink_factor: bfloat16 [128, 8192, 128], P('groups', 'fsdp'), parts along dimension 0, may hold values from -0.0625 to 0.0625
- expand_factor: bfloat16 [128, 128, 1024], P('groups', 'fsdp'), parts along dimension 0, may hold values from -0.5 to 0.5
- rank_per_adapter: int32 [128], P('groups'), parts along dimension 0, may hold values from 16 to 128, as said below
- block_adapter: int32 [32], P('groups'), parts along dimension 0, may hold values from 0 to 63
- block_rows: int32 [32], P(('groups', 'fsdp')), parts along dimension 0, may hold values from 32 to 128, as said below
Outputs:
- projected: bfloat16 [4096, 1024], P(('groups', 'fsdp')), parts along dimension 0
- token_input_gradient: bfloat16 [4096, 8192], P(('groups', 'fsdp')), parts along dimension 0
- shrink_grad: float32 [128, 8192, 128], P('groups', 'fsdp'), parts along dimension 0
- expand_grad: float32 [128, 128, 1024], P('groups', 'fsdp'), parts along dimension 0
There are 2 independent parts, one for each index of `groups`. A program takes and returns all parts, laid end to end along the dimension named above; an argument that names none is the same for every part. Nothing has to cross between parts.
Inputs may be any that keep to these rules, and one draw needn't show every extreme that they name: `rank_per_adapter`: every rank is a power of two; some adapter has rank 128 and some has rank 16. `block_rows`: some block has all 128 rows valid and some has 32.
All inputs are finite; a program needn't handle non-finite values.
Results may differ from a plain program's by a relative error of at most 0.0044.
Values may be sent and summed in bfloat16 or wider, within the bound.
No kernel may reach another device: no remote copies, remote signals or barrier semaphores. Data moves between devices by JAX's collectives and lax.ppermute only.
A program may use at most 128 MiB of HBM per device.

v0:
```python
import jax
import jax.numpy as jnp
from jax import lax
from jax.sharding import PartitionSpec as P

ADAPTERS = 64
BLOCK = 128


ADAPTER_STRENGTH = 16.0


def block_terms(x_block, e_block, in_factor, out_factor, scaling, rank_now, columns):
    kept_cols = lax.iota(jnp.int32, columns)[None, :] < rank_now
    shrink = jnp.dot(x_block, in_factor, preferred_element_type=jnp.float32)
    shrink = jnp.where(kept_cols, shrink, 0.0).astype(jnp.bfloat16)
    expand_matrix = jnp.dot(shrink, out_factor, preferred_element_type=jnp.float32) * scaling
    back_grad = (
        lax.dot_general(
            e_block, out_factor, (((1,), (1,)), ((), ())), preferred_element_type=jnp.float32
        )
        * scaling
    )
    back_grad = jnp.where(kept_cols, back_grad, 0.0).astype(jnp.bfloat16)
    input_portion = lax.dot_general(
        back_grad, in_factor, (((1,), (1,)), ((), ())), preferred_element_type=jnp.float32
    )
    gradient_down = lax.dot_general(
        x_block, back_grad, (((0,), (0,)), ((), ())), preferred_element_type=jnp.float32
    )
    grad_out_f = (
        lax.dot_general(
            shrink, e_block, (((0,), (0,)), ((), ())), preferred_element_type=jnp.float32
        )
        * scaling
    )
    return (expand_matrix, input_portion, back_grad, gradient_down, grad_out_f)


def on_device(
    tokens,
    grad_out,
    base_weight,
    shrink_factor,
    expand_factor,
    rank_per_adapter,
    block_adapter,
    block_rows,
):
    tok_rows, model_width = tokens.shape
    rank_cap = shrink_factor.shape[2]
    local_blocks = tok_rows // BLOCK
    my_index = lax.axis_index("fsdp")
    own_ids = lax.dynamic_slice_in_dim(block_adapter, my_index * local_blocks, local_blocks)
    row_valid = (lax.iota(jnp.int32, BLOCK)[None, :] < block_rows[:, None]).reshape(tok_rows, 1)
    masked = jnp.where(row_valid, grad_out, jnp.zeros((), grad_out.dtype))
    send_in = jnp.take(shrink_factor, block_adapter, axis=0)
    send_up = jnp.take(expand_factor, block_adapter, axis=0)
    full_in, full_up = (
        lax.all_to_all(send_in, "fsdp", split_axis=0, concat_axis=1, tiled=True),
        lax.all_to_all(send_up, "fsdp", split_axis=0, concat_axis=1, tiled=True),
    )
    full_weight = lax.all_gather(base_weight, "fsdp", axis=0, tiled=True)
    frozen_output = jnp.dot(tokens, full_weight, preferred_element_type=jnp.float32)
    frozen_backward = lax.dot_general(
        masked, full_weight, (((1,), (1,)), ((), ())), preferred_element_type=jnp.float32
    )
    adapter_scales = ADAPTER_STRENGTH / jnp.sqrt(rank_per_adapter.astype(jnp.float32))
    adapter_iota = lax.iota(jnp.int32, ADAPTERS)
    expands, input_parts, back_list, grad_in_list, grad_up_list = ([], [], [], [], [])
    picked = adapter_iota == own_ids[0]
    scaling = jnp.sum(jnp.where(picked, adapter_scales, 0.0))
    rank_now = jnp.sum(jnp.where(picked, rank_per_adapter, 0))
    results = block_terms(tokens, masked, full_in[0], full_up[0], scaling, rank_now, rank_cap)
    expands.append(results[0])
    input_parts.append(results[1])
    back_list.append(results[2])
    grad_in_list.append(results[3])
    grad_up_list.append(results[4])
    projected = (frozen_output + expands[0]).astype(jnp.bfloat16)
    token_input_gradient = (frozen_backward + input_parts[0]).astype(jnp.bfloat16)
    grad_up_all = jnp.stack(grad_up_list, axis=0)
    onehot = (adapter_iota[:, None] == block_adapter[None, :]).astype(jnp.float32)
    grad_in_all = jnp.stack(grad_in_list, axis=0)
    recv_in, recv_up = (
        lax.all_to_all(grad_in_all, "fsdp", split_axis=1, concat_axis=0, tiled=True),
        lax.all_to_all(grad_up_all, "fsdp", split_axis=1, concat_axis=0, tiled=True),
    )
    shrink_grad = jnp.einsum("ab,bdr->adr", onehot, recv_in, precision=lax.Precision.HIGHEST)
    expand_grad = jnp.einsum("ab,brk->ark", onehot, recv_up, precision=lax.Precision.HIGHEST)
    return (projected, token_input_gradient, shrink_grad, expand_grad)


def solution(mesh):
    placed = (
        P(("groups", "fsdp"), None),
        P(("groups", "fsdp"), None),
        P("fsdp", None),
        P("groups", "fsdp", None),
        P("groups", "fsdp", None),
        P("groups"),
        P("groups"),
        P(("groups", "fsdp")),
    )
    return jax.shard_map(
        on_device,
        mesh=mesh,
        in_specs=placed,
        out_specs=(
            P(("groups", "fsdp"), None),
            P(("groups", "fsdp"), None),
            P("groups", "fsdp", None),
            P("groups", "fsdp", None),
        ),
        check_vma=False,
    )
```

profile of v0, /device:TPU:11, one launch (start us, length us, event | category | flops | bytes accessed | tf_op | source)
XLA Modules:
  0.0 341.8 jit_solution(17087939189502092844)
XLA Ops:
  7.2 0.7 all-gather.2.cloned.1.call-update
  7.9 0.7 compare_select_fusion
  8.6 5.5 %gather_fusion = bf16[16,512,128]{2,1,0:T(8,128)(2,1)} fusion(bf16[64,512,128]{2,1,0:T(8,128)(2,1)} %param.11, s32[1024]{0:T(1024)S(1)} %pad_clamp_fusion), kind=kCustom, calls=%fused_computation | custom fusion | bytes 4194368 | tf_op jit(solution)/shard_map/jit(_take)/gather | solution.py:57
  14.1 3.2 broadcast_select_fusion
  17.3 6.7 %all-to-all-start = ((bf16[16,512,128]{2,1,0:T(8,128)(2,1)}), bf16[16,512,128]{2,1,0:T(8,128)(2,1)}, u32[]{:S(2)}, u32[]{:S(2)}) async-start(bf16[16,512,128]{2,1,0:T(8,128)(2,1)} %broadcast_select_fusion), calls=%async_computation | async-start | bytes 4194304 | tf_op jit(solution)/shard_map/all_to_all | solution.py:60
  24.6 0.6 dynamic_slice.3
  25.2 1.8 gather_fusion.1
  27.0 1.3 fusion.18
  28.3 1.2 fusion.19
  29.6 0.8 broadcast_select_fusion.2
  30.4 71.9 %all-to-all-done = bf16[16,512,128]{2,1,0:T(8,128)(2,1)} async-done(((bf16[16,512,128]{2,1,0:T(8,128)(2,1)}), bf16[16,512,128]{2,1,0:T(8,128)(2,1)}, u32[]{:S(2)}, u32[]{:S(2)}) %all-to-all-start) | async-done | bytes 2097184 | tf_op jit(solution)/shard_map/all_to_all | solution.py:60
  102.2 4.6 %all-to-all-start.1 = ((bf16[16,8,1024]{2,1,0:T(8,128)(2,1)}), bf16[16,8,1024]{2,1,0:T(8,128)(2,1)S(1)}, u32[]{:S(2)}, u32[]{:S(2)}) async-start(bf16[16,8,1024]{2,1,0:T(8,128)(2,1)} %broadcast_select_fusion.2), calls=%async_computation.1 | async-start | bytes 524288 | tf_op jit(solution)/shard_map/all_to_all | solution.py:61
  106.8 0.6 iota_compare_fusion.1
  107.5 2.5 fusion.8
  110.0 0.8 fusion.3
  110.8 1.3 copy.22
  112.1 11.2 %all-to-all-done.1 = bf16[16,8,1024]{2,1,0:T(8,128)(2,1)S(1)} async-done(((bf16[16,8,1024]{2,1,0:T(8,128)(2,1)}), bf16[16,8,1024]{2,1,0:T(8,128)(2,1)S(1)}, u32[]{:S(2)}, u32[]{:S(2)}) %all-to-all-start.1) | async-done | bytes 262176 | tf_op jit(solution)/shard_map/all_to_all | solution.py:61
  123.4 4.1 %all-to-all-start.3 = ((f32[1,128,1024]{2,0,1:T(1,128)}), f32[1,128,1024]{2,0,1:T(1,128)S(1)}, u32[]{:S(2)}, u32[]{:S(2)}) async-start(f32[1,128,1024]{2,0,1:T(1,128)} %copy.22), calls=%async_computation.3 | async-start | bytes 1048576 | tf_op jit(solution)/shard_map/all_to_all | solution.py:87
  127.5 0.8 fusion.7
  128.3 2.8 convolution_bitcast_fusion
  131.0 9.7 %copy.20 = f32[1,8192,128]{2,0,1:T(1,128)} copy(f32[1,8192,128]{1,2,0:T(8,128)} %convolution_bitcast_fusion) | data formatting | bytes 8388608 | tf_op jit(solution)/shard_map/stack | solution.py:84
  140.7 15.0 %all-to-all-done.3 = f32[1,128,1024]{2,0,1:T(1,128)S(1)} async-done(((f32[1,128,1024]{2,0,1:T(1,128)}), f32[1,128,1024]{2,0,1:T(1,128)S(1)}, u32[]{:S(2)}, u32[]{:S(2)}) %all-to-all-start.3) | async-done | bytes 524320 | tf_op jit(solution)/shard_map/all_to_all | solution.py:87
  155.7 6.4 %all-to-all-start.2 = ((f32[1,8192,128]{2,0,1:T(1,128)}), f32[1,8192,128]{2,0,1:T(1,128)}, u32[]{:S(2)}, u32[]{:S(2)}) async-start(f32[1,8192,128]{2,0,1:T(1,128)} %copy.20), calls=%async_computation.2 | async-start | bytes 8388608 | tf_op jit(solution)/shard_map/all_to_all | solution.py:86
  162.2 1.2 fusion.9
  163.4 2.5 copy.25
  165.9 111.0 %all-to-all-done.2 = f32[1,8192,128]{2,0,1:T(1,128)} async-done(((f32[1,8192,128]{2,0,1:T(1,128)}), f32[1,8192,128]{2,0,1:T(1,128)}, u32[]{:S(2)}, u32[]{:S(2)}) %all-to-all-start.2) | async-done | bytes 4194336 | tf_op jit(solution)/shard_map/all_to_all | solution.py:86
  276.9 10.8 %fusion.1 = f32[64,512,128]{2,0,1:T(8,128)S(1)} fusion(f32[16,512,128]{2,1,0:T(8,128)} %bitcast.7, s32[16]{0:T(128)S(1)} %copy-done.2), kind=kOutput, calls=%fused_computation.5 | convolution fusion | flops 805307392 | bytes 20971584 | tf_op jit(solution)/shard_map/ab,bdr->adr/dot_general | solution.py:89
  287.8 19.4 %copy.24 = f32[64,512,128]{2,1,0:T(8,128)} copy(f32[64,512,128]{2,0,1:T(8,128)S(1)} %fusion.1) | data formatting | bytes 33554432
  307.1 13.3 %fusion.20 = f32[128,8192]{1,0:T(8,128)} fusion(bf16[8192,1024]{1,0:T(8,128)(2,1)} %all-gather.2.cloned.1.call-done, bf16[128,1024]{1,0:T(8,128)(2,1)S(1)} %copy-done.1, pred[128]{0:T(512)(128)(4,1)S(1)} %get-tuple-element.16), kind=kOutput, calls=%fused_computation.38 | convolution fusion | flops 2147614720 | bytes 21233792 | tf_op jit(solution)/shard_map/dot_general | solution.py:65
  320.4 4.9 %fusion = bf16[128,8192]{1,0:T(8,128)(2,1)} fusion(f32[128,8192]{1,0:T(8,128)} %fusion.20, bf16[128,128]{1,0:T(8,128)(2,1)S(1)} %fusion.7, bf16[8192,128]{1,0:T(8,128)(2,1)} %bitcast.1), kind=kOutput, calls=%fused_computation.4 | convolution fusion | flops 270532608 | bytes 8421376 | tf_op jit(solution)/shard_map/dot_general | solution.py:25
  325.3 8.1 %fusion.21 = f32[128,1024]{1,0:T(8,128)S(1)} fusion(bf16[128,8192]{1,0:T(8,128)(2,1)S(1)} %copy-done, bf16[8192,1024]{1,0:T(8,128)(2,1)} %all-gather.2.cloned.1.call-done), kind=kOutput, calls=%fused_computation.39 | convolution fusion | flops 2147483648 | bytes 19398656 | tf_op jit(solution)/shard_map/dot_general | solution.py:64
  333.4 1.5 fusion.5
  (13 shorter events, 0.2 us)
Async XLA Ops:
  7.2 100.3 %copy-start = (bf16[128,8192]{1,0:T(8,128)(2,1)S(1)}, bf16[128,8192]{1,0:T(8,128)(2,1)}, u32[]{:S(2)}) copy-start(bf16[128,8192]{1,0:T(8,128)(2,1)} %param.8) | copy-start | bytes 6291460
  7.2 299.9 %all-gather.2.cloned.1.call-start = ((), (), s32[]{:S(2)}) async-start(), calls=%async_computation.4 | async-start | bytes 17825792 | tf_op jit(solution)/shard_map/all_gather | solution.py:63
  8.6 5.5 %copy-start.2 = (s32[16]{0:T(128)S(1)}, s32[16]{0:T(128)}, u32[]{:S(2)}) copy-start(s32[16]{0:T(128)} %param.14) | copy-start | bytes 196
  17.3 9.7 %copy-start.3 = (s32[64]{0:T(128)S(1)}, s32[64]{0:T(128)}, u32[]{:S(2)}) copy-start(s32[64]{0:T(128)} %param.13) | copy-start | bytes 772
  17.3 84.9 %all-to-all-start = ((bf16[16,512,128]{2,1,0:T(8,128)(2,1)}), bf16[16,512,128]{2,1,0:T(8,128)(2,1)}, u32[]{:S(2)}, u32[]{:S(2)}) async-start(bf16[16,512,128]{2,1,0:T(8,128)(2,1)} %broadcast_select_fusion), calls=%async_computation | async-start | bytes 4194304 | tf_op jit(solution)/shard_map/all_to_all | solution.py:60
  102.2 21.2 %all-to-all-start.1 = ((bf16[16,8,1024]{2,1,0:T(8,128)(2,1)}), bf16[16,8,1024]{2,1,0:T(8,128)(2,1)S(1)}, u32[]{:S(2)}, u32[]{:S(2)}) async-start(bf16[16,8,1024]{2,1,0:T(8,128)(2,1)} %broadcast_select_fusion.2), calls=%async_computation.1 | async-start | bytes 524288 | tf_op jit(solution)/shard_map/all_to_all | solution.py:61
  107.5 2.5 copy-start.1
  123.4 32.3 %all-to-all-start.3 = ((f32[1,128,1024]{2,0,1:T(1,128)}), f32[1,128,1024]{2,0,1:T(1,128)S(1)}, u32[]{:S(2)}, u32[]{:S(2)}) async-start(f32[1,128,1024]{2,0,1:T(1,128)} %copy.22), calls=%async_computation.3 | async-start | bytes 1048576 | tf_op jit(solution)/shard_map/all_to_all | solution.py:87
  155.7 121.2 %all-to-all-start.2 = ((f32[1,8192,128]{2,0,1:T(1,128)}), f32[1,8192,128]{2,0,1:T(1,128)}, u32[]{:S(2)}, u32[]{:S(2)}) async-start(f32[1,8192,128]{2,0,1:T(1,128)} %copy.20), calls=%async_computation.2 | async-start | bytes 8388608 | tf_op jit(solution)/shard_map/all_to_all | solution.py:86
Sparse Core Ops, SparseCore 0:
  10.2 233.1 all-gather.1
where the time goes:
time: 343 us; the launch traced here: 342 us
  waiting for transfers between devices  210 us (61%)
  matrix products  46.6 us (14%)
  local copies, waits for them, and re-layouts  40.9 us (12%)
  starting transfers between devices  21.8 us (6%)
  between operations  14.8 us (4%)
  other arithmetic  7.82 us (2%)
    all_to_all x1, waiting for transfers between devices, on_device(): lax.all_to_all(grad_in_all, 'fsdp', split_axis=1, concat_axis=0, tiled=True)  111 us
    all_to_all x1, waiting for transfers between devices, on_device(): lax.all_to_all(send_in, 'fsdp', split_axis=0, concat_axis=1, tiled=True)  71.9 us
    unnamed x11, local copies, waits for them, and re-layouts  22 us
    all_to_all x1, waiting for transfers between devices, on_device(): lax.all_to_all(grad_up_all, 'fsdp', split_axis=1, concat_axis=0, tiled=True)  15 us
    dot_general x1, matrix products, on_device(): lax.dot_general(masked, full_weight, (((1,), (1,)), ((), ())), preferred_...  13.3 us
    all_to_all x1, waiting for transfers between devices, on_device(): lax.all_to_all(send_up, 'fsdp', split_axis=0, concat_axis=1, tiled=True)  11.2 us
    dot_general x1, matrix products, on_device(): jnp.einsum('ab,bdr->adr', onehot, recv_in, precision=lax.Precision.HIGHEST)  10.8 us
    another operation x1, local copies, waits for them, and re-layouts, on_device(): grad_in_all = jnp.stack(grad_in_list, axis=0)  9.68 us
  transfers between devices with their start and end apart: 5, of which 4 were waited for; matrix products, arithmetic and copies ran while one was open for 20% of the time, Pallas kernels for 0%

commit v1 on v0

v1 whole, which is shorter than its diff:
```python
import jax
import jax.numpy as jnp
from jax import lax
from jax.experimental import pallas as pl
from jax.experimental.pallas import tpu as pltpu
from jax.sharding import PartitionSpec as P

BLOCK = 128
ADAPTER_STRENGTH = 16.0
INNER = 4
MIB = 1 << 20
BF = jnp.bfloat16
F32 = jnp.float32

HBM = pl.BlockSpec(memory_space=pltpu.HBM)
VM = pl.BlockSpec(memory_space=pltpu.VMEM)
SM = pl.BlockSpec(memory_space=pltpu.SMEM)


def params(mib):
    return pltpu.CompilerParams(vmem_limit_bytes=mib * MIB)


COST = pl.CostEstimate(flops=1, bytes_accessed=1, transcendentals=0)


def dot(a, b, ca, cb):
    return lax.dot_general(a, b, (((ca,), (cb,)), ((), ())), preferred_element_type=F32)


def adapter_scale(rank):
    return ADAPTER_STRENGTH / jnp.sqrt(jnp.full((BLOCK, BLOCK), rank, jnp.int32).astype(F32))


def pick_kernel(outer, me_ref, ids_ref, factor, s_send, s_keep, sem):
    def start(i, carry):
        core = lax.div(i, outer)
        own = jnp.bitwise_xor(me_ref[0], lax.rem(i, outer) * INNER + core)
        pltpu.make_async_copy(factor.at[ids_ref[own]], s_keep.at[i], sem.at[0]).start()
        far = jnp.bitwise_xor(own, 2)
        pltpu.make_async_copy(factor.at[ids_ref[far]], s_send.at[i], sem.at[1]).start()
        return carry

    half = s_keep.shape[0]
    lax.fori_loop(0, half, start, 0)
    pltpu.make_async_copy(factor.at[pl.ds(0, half)], s_keep, sem.at[0]).wait()
    pltpu.make_async_copy(factor.at[pl.ds(0, half)], s_send, sem.at[1]).wait()


def pick(me, ids, factor, outer):
    picked = jax.ShapeDtypeStruct((2 * outer,) + factor.shape[1:], BF)
    return pl.pallas_call(
        lambda *refs: pick_kernel(outer, *refs),
        out_shape=(picked, picked),
        in_specs=[SM, SM, HBM],
        out_specs=(VM, VM),
        scratch_shapes=[pltpu.SemaphoreType.DMA((2,))],
        compiler_params=params(57),
        cost_estimate=COST,
        name="pick_factors",
    )(me, ids, factor)


def first_kernel(outer, me_ref, ids_ref, ranks_ref, rows_ref, tokens, grad, up_ref, *outs):
    rank = ranks_ref[ids_ref[me_ref[0]]]
    plane = lax.div(me_ref[0], INNER)
    dz = tokens.shape[1] // outer
    kv = grad.shape[1]
    rows = lax.broadcasted_iota(jnp.int32, grad.shape, 0)
    masked = jnp.where(rows < rows_ref[0], grad[...].astype(F32), 0.0).astype(BF)
    back = dot(masked, up_ref[...], 1, 1) * adapter_scale(rank)
    cols = lax.broadcasted_iota(jnp.int32, back.shape, 1)
    back = jnp.where(cols < rank, back, 0.0).astype(BF)
    for k, out in enumerate(outs):
        at = pl.multiple_of(jnp.bitwise_xor(plane, k) * dz, dz)
        out[:, :dz] = tokens[:, pl.ds(at, dz)]
        out[:, dz : dz + kv] = masked
        out[:, dz + kv :] = back


def first_sends(me, ids, ranks, block_rows, tokens, grad, up, outer):
    rows, width = tokens.shape
    wide = width // outer + grad.shape[1] + up.shape[0]
    return pl.pallas_call(
        lambda *refs: first_kernel(outer, *refs),
        out_shape=tuple(jax.ShapeDtypeStruct((rows, wide), BF) for _ in range(outer)),
        in_specs=[SM] * 4 + [VM] * 3,
        out_specs=(VM,) * outer,
        compiler_params=params(24),
        cost_estimate=COST,
        name="first_sends",
    )(me, ids, ranks, block_rows, tokens, grad, up)


def plane_parts(me, w, s, scratch, outer, sub):
    own = lax.rem(me, INNER)
    parts = []
    for j, (ws, (ref, at)) in enumerate(zip(w, s)):
        first = pl.multiple_of(jnp.bitwise_xor(own, j) * sub, sub)
        row = 0
        for weight in ws:
            size = weight.shape[0]
            rows = slice(row, row + size)
            if scratch:
                wz, sz = scratch
                base = pl.multiple_of(first + row, size)
                wz[pl.ds(base, size), :] = weight[...]
                for k in range(outer):
                    sz[k, pl.ds(base, size), :] = ref[at + k, rows, :]
            else:
                base = pl.multiple_of(first + row, size)
                factors = [ref.at[at + k, rows] for k in range(outer)]
                parts.append((base, size, weight, factors))
            row += size
    if scratch:
        wz, sz = scratch
        parts = [(0, wz.shape[0], wz, [sz.at[k] for k in range(outer)])]
    return parts


def plane_scratch(outer, sub, kv, rank):
    if sub % 256 == 0:
        return []
    dz = sub * INNER
    return [pltpu.VMEM((dz, kv), BF), pltpu.VMEM((outer, dz, rank), BF)]


def main_kernel(outer, sub, kv, me_ref, *refs):
    w = [[refs[0]], [refs[1]], [refs[2]], [refs[3], refs[4]]]
    s = [(refs[5], 0), (refs[7], 0), (refs[6], 0), (refs[8], 0)]
    xe = refs[9 : 9 + outer]
    held_t, held_f = refs[9 + outer : 11 + outer]
    sends = refs[11 + outer : 10 + 2 * outer]
    x, e, *scratch = refs[10 + 2 * outer :]
    dz = sub * INNER
    for k in range(outer):
        x[k * BLOCK : (k + 1) * BLOCK, :] = xe[k][:, :dz]
        e[k * BLOCK : (k + 1) * BLOCK, :] = xe[k][:, dz : dz + kv]
    parts = plane_parts(me_ref[0], w, s, scratch, outer, sub)
    for first, size, weight, factors in parts:
        base = dot(e[...], weight[...], 1, 1)
        for k in range(outer):
            extra = dot(xe[k][:, dz + kv :], factors[k][...], 1, 1)
            out = held_t if k == 0 else sends[k - 1]
            rows = slice(k * BLOCK, (k + 1) * BLOCK)
            out[:, pl.ds(first, size)] = (base[rows] + extra).astype(BF)
    step = 256
    for c in range(0, kv, step):
        part = sum(
            dot(x[:, pl.ds(first, size)], weight[:, c : c + step], 1, 0)
            for first, size, weight, _ in parts
        )
        held_f[:, c : c + step] = part[:BLOCK]
        for k in range(1, outer):
            rows = slice(k * BLOCK, (k + 1) * BLOCK)
            sends[k - 1][:, dz + c : dz + c + step] = part[rows].astype(BF)


def main_parts(me, wparts, sparts, xe, outer):
    sub, kv = wparts[0].shape
    rank = sparts[0].shape[-1]
    dz = sub * INNER
    return pl.pallas_call(
        lambda *refs: main_kernel(outer, sub, kv, *refs),
        out_shape=(
            jax.ShapeDtypeStruct((BLOCK, dz), BF),
            jax.ShapeDtypeStruct((BLOCK, kv), F32),
        )
        + tuple(jax.ShapeDtypeStruct((BLOCK, dz + kv), BF) for _ in range(outer - 1)),
        in_specs=[SM] + [VM] * (9 + outer),
        out_specs=(VM,) * (1 + outer),
        scratch_shapes=[
            pltpu.VMEM((outer * BLOCK, dz), BF),
            pltpu.VMEM((outer * BLOCK, kv), BF),
        ]
        + plane_scratch(outer, sub, kv, rank),
        compiler_params=params(48),
        cost_estimate=COST,
        name="plane_products",
    )(me, *wparts, *sparts, *xe)


def shrink_kernel(outer, sub, me_ref, *refs):
    s = [refs[0], refs[2], refs[1], refs[3]]
    xe = refs[4 : 4 + outer]
    outs = refs[4 + outer : 4 + 2 * outer]
    scratch = refs[4 + 2 * outer :]
    own = lax.rem(me_ref[0], INNER)
    for k in range(outer):
        total = None
        for j, ref in enumerate(s):
            first = pl.multiple_of(jnp.bitwise_xor(own, j) * sub, sub)
            if scratch:
                scratch[0][pl.ds(first, sub), :] = ref[k]
            else:
                term = dot(xe[k][:, pl.ds(first, sub)], ref[k], 1, 0)
                total = term if total is None else total + term
        if scratch:
            total = dot(xe[k][:, : sub * INNER], scratch[0][...], 1, 0)
        outs[k][...] = total


def shrink_parts(me, sparts, xe, outer):
    sub, rank = sparts[0].shape[1:]
    scratch = [] if sub % 128 == 0 else [pltpu.VMEM((sub * INNER, rank), BF)]
    return pl.pallas_call(
        lambda *refs: shrink_kernel(outer, sub, *refs),
        out_shape=tuple(jax.ShapeDtypeStruct((BLOCK, rank), F32) for _ in range(outer)),
        in_specs=[SM] + [VM] * (4 + outer),
        out_specs=(VM,) * outer,
        scratch_shapes=scratch,
        compiler_params=params(24),
        cost_estimate=COST,
        name="shrink_parts",
    )(me, *sparts, *xe)


def rows_kernel(outer, dz, me_ref, ids_ref, ranks_ref, *refs):
    parts = refs[:outer]
    up, own, extra, eg = refs[outer:]
    rank = ranks_ref[ids_ref[me_ref[0]]]
    low = sum(p[...] for p in parts)
    cols = lax.broadcasted_iota(jnp.int32, low.shape, 1)
    shrink = jnp.where(cols < rank, low, 0.0).astype(BF)
    scale = adapter_scale(rank)[:, :1]
    extra[...] = dot(shrink, up[...], 1, 0) * scale
    kv = up.shape[1]
    eg[...] = (dot(shrink, own[:, dz : dz + kv], 0, 0) * scale).astype(BF)


def shrunk_rows(me, ids, ranks, parts, up, own):
    rank_cap, kv = up.shape
    outer = len(parts)
    return pl.pallas_call(
        lambda *refs: rows_kernel(outer, own.shape[1] - kv - rank_cap, *refs),
        out_shape=(
            jax.ShapeDtypeStruct((BLOCK, kv), F32),
            jax.ShapeDtypeStruct((rank_cap, kv), BF),
        ),
        in_specs=[SM, SM, SM] + [VM] * (outer + 2),
        out_specs=(VM, VM),
        compiler_params=params(24),
        cost_estimate=COST,
        name="shrunk_rows",
    )(me, ids, ranks, *parts, up, own)


def pack_kernel(outer, sub, rank, me_ref, *refs):
    xe, outs = refs[:outer], refs[outer:]
    own = lax.rem(me_ref[0], INNER)
    last = xe[0].shape[1] - rank
    for j, out in enumerate(outs):
        for k in range(outer):
            out[k * BLOCK : (k + 1) * BLOCK, :rank] = xe[k][:, last:]
        for quarter in range(INNER):

            @pl.when(jnp.bitwise_xor(own, j) == quarter)
            def _(quarter=quarter, out=out):
                for k in range(outer):
                    part = xe[k][:, quarter * sub : (quarter + 1) * sub]
                    out[k * BLOCK : (k + 1) * BLOCK, rank:] = part


def pack(me, xe, sub, rank, outer):
    shape = jax.ShapeDtypeStruct((outer * BLOCK, rank + sub), BF)
    return pl.pallas_call(
        lambda *refs: pack_kernel(outer, sub, rank, *refs),
        out_shape=(shape,) * INNER,
        in_specs=[SM] + [VM] * outer,
        out_specs=(VM,) * INNER,
        compiler_params=params(24),
        cost_estimate=COST,
        name="pack_columns",
    )(me, *xe)


def down_kernel(per, blocks, rank, me_ref, ids_ref, *refs):
    out = refs[-1]
    first = pl.program_id(0) * per
    out[...] = jnp.zeros_like(out)

    for j, ref in enumerate(refs[:-1]):

        def each(k, carry, ref=ref, j=j):
            slot = ids_ref[jnp.bitwise_xor(me_ref[0], k * INNER + j)] - first

            @pl.when(jnp.logical_and(slot >= 0, slot < per))
            def _():
                rows = pl.ds(pl.multiple_of(k * BLOCK, BLOCK), BLOCK)
                out[slot] += dot(ref[rows, rank:], ref[rows, :rank], 0, 0)

            return carry

        lax.fori_loop(0, blocks, each, 0)


def down_grad(me, ids, packed, adapters, rank):
    shape = packed[0].shape
    sub = shape[1] - rank
    blocks = shape[0] // BLOCK
    per = 4
    whole = pl.BlockSpec(shape, lambda i, *_: (0, 0))
    return pl.pallas_call(
        lambda *refs: down_kernel(per, blocks, rank, *refs),
        grid_spec=pltpu.PrefetchScalarGridSpec(
            num_scalar_prefetch=2,
            grid=(adapters // per,),
            in_specs=[whole] * len(packed),
            out_specs=pl.BlockSpec((per, sub, rank), lambda i, *_: (i, 0, 0)),
        ),
        out_shape=jax.ShapeDtypeStruct((adapters, sub, rank), F32),
        compiler_params=params(32),
        cost_estimate=COST,
        name="down_gradient",
    )(me, ids, *packed)


def up_kernel(per, blocks, ids_ref, got, out):
    first = pl.program_id(0) * per
    out[...] = jnp.zeros_like(out)

    def each(i, carry):
        slot = ids_ref[i] - first

        @pl.when(jnp.logical_and(slot >= 0, slot < per))
        def _():
            out[slot] += got[i].astype(F32)

        return carry

    lax.fori_loop(0, blocks, each, 0)


def up_grad(ids, got, adapters):
    blocks, part, kv = got.shape
    per = 16
    return pl.pallas_call(
        lambda *refs: up_kernel(per, blocks, *refs),
        grid_spec=pltpu.PrefetchScalarGridSpec(
            num_scalar_prefetch=1,
            grid=(adapters // per,),
            in_specs=[pl.BlockSpec(got.shape, lambda i, *_: (0, 0, 0))],
            out_specs=pl.BlockSpec((per, part, kv), lambda i, *_: (i, 0, 0)),
        ),
        out_shape=jax.ShapeDtypeStruct((adapters, part, kv), F32),
        compiler_params=params(24),
        cost_estimate=COST,
        name="up_gradient",
    )(ids, got)


def join_kernel(outer, dz, me_ref, held_t, held_f, extra, *refs):
    got, proj, grad = refs[:-2], refs[-2], refs[-1]
    plane = lax.div(me_ref[0], INNER)
    for k in range(outer):
        at = pl.multiple_of(jnp.bitwise_xor(plane, k) * dz, dz)
        grad[:, pl.ds(at, dz)] = held_t[...] if k == 0 else got[k - 1][:, :dz]
    total = held_f[...] + extra[...] + sum(g[:, dz:].astype(F32) for g in got)
    proj[...] = total.astype(BF)


def join(me, held_t, held_f, extra, got):
    rows, dz = held_t.shape
    outer = 1 + len(got)
    return pl.pallas_call(
        lambda *refs: join_kernel(outer, dz, *refs),
        out_shape=(
            jax.ShapeDtypeStruct(held_f.shape, BF),
            jax.ShapeDtypeStruct((rows, dz * outer), BF),
        ),
        in_specs=[SM] + [VM] * (2 + outer),
        out_specs=(VM, VM),
        compiler_params=params(24),
        cost_estimate=COST,
        name="join_columns",
    )(me, held_t, held_f, extra, *got)


def build(devices):
    outer = devices // INNER

    def swap(value, mask):
        return lax.ppermute(value, "fsdp", [(i, i ^ mask) for i in range(devices)])

    def on_device(tokens, grad_out, base_weight, shrink_factor, expand_factor,
                  rank_per_adapter, block_adapter, block_rows):
        adapters, sub, rank = shrink_factor.shape
        kv = base_weight.shape[1]
        me = lax.axis_index("fsdp").reshape(1).astype(jnp.int32)

        def after(value, earlier):
            return lax.optimization_barrier((value, earlier))[0]

        def to_planes(parts):
            got = {k: swap(parts[k], k * INNER) for k in reversed(range(1, outer))}
            return [parts[0]] + [got[k] for k in range(1, outer)]

        up_send = jnp.take(expand_factor, block_adapter, axis=0, mode="clip")
        up = lax.all_to_all(up_send, "fsdp", split_axis=0, concat_axis=0, tiled=True)
        up = up.reshape(rank, kv)

        s_send, s_keep = pick(me, after(block_adapter, up_send), shrink_factor, outer)
        s_x = swap(after(s_send, up), 2)
        w_x = swap(after(base_weight, up), 2)
        s_c = swap(s_keep[outer:], 1)
        s_xc = swap(s_x[outer:], 1)
        w_c = swap(base_weight, 1)
        w_xc = [swap(w_x[: sub // 2], 1), swap(w_x[sub // 2 :], 1)]
        wparts = (base_weight, w_c, w_x, *w_xc)
        sparts = (s_keep, s_x, s_c, s_xc)

        cuts = first_sends(
            me, block_adapter, rank_per_adapter, block_rows, tokens, grad_out,
            after(up, s_keep), outer,
        )
        xe = to_planes(cuts)

        low = shrink_parts(me, sparts, xe, outer)
        held_t, held_f, *sends = main_parts(me, wparts, sparts, after(xe, low), outer)
        low = to_planes(low)
        extra, eg = shrunk_rows(
            me, block_adapter, rank_per_adapter, after(low, sends), up, cuts[0]
        )
        eg_got = eg.reshape(devices, rank // devices, kv)
        eg_got = lax.all_to_all(eg_got, "fsdp", split_axis=0, concat_axis=0, tiled=True)

        packed = pack(me, after(xe, eg), sub, rank, outer)
        packed = [p if j == 0 else swap(p, j) for j, p in enumerate(packed)]
        shrink_grad = down_grad(me, block_adapter, packed, adapters, rank)
        expand_grad = up_grad(after(block_adapter, shrink_grad), eg_got, adapters)
        got = to_planes([held_t] + sends)[1:]
        projected, token_input_gradient = join(
            me, held_t, held_f, extra, after(got, expand_grad)
        )
        return (projected, token_input_gradient, shrink_grad, expand_grad)

    return on_device


def solution(mesh):
    placed = (
        P(("groups", "fsdp"), None),
        P(("groups", "fsdp"), None),
        P("fsdp", None),
        P("groups", "fsdp", None),
        P("groups", "fsdp", None),
        P("groups"),
        P("groups"),
        P(("groups", "fsdp")),
    )
    return jax.shard_map(
        build(mesh.shape["fsdp"]),
        mesh=mesh,
        in_specs=placed,
        out_specs=(
            P(("groups", "fsdp"), None),
            P(("groups", "fsdp"), None),
            P("groups", "fsdp", None),
            P("groups", "fsdp", None),
        ),
        check_vma=False,
    )
```

time: 343 us -> 201 us (0.59)
  waiting for transfers between devices: 210 us -> 111 us
  matrix products: 46.6 us -> 0 us
  Pallas kernels: 0 us -> 39.2 us
  local copies, waits for them, and re-layouts: 40.9 us -> 6.05 us
  starting transfers between devices: 21.8 us -> 40.2 us
  between operations: 14.8 us -> 1.62 us
  other arithmetic: 7.82 us -> 0.75 us
    all_to_all x4 -> x2, waiting for transfers between devices: 209 us -> 31.1 us  [the longest x1 26.9 us: on_device(): lax.all_to_all(eg_got, 'fsdp', split_axis=0, concat_axis=0, tiled=True)]
    ppermute x0 -> x19, waiting for transfers between devices: none -> 79.7 us  [swap(): return lax.ppermute(value, 'fsdp', [(i, i ^ mask) for i in range(devices)])]
    dot_general x10 -> x0, matrix products: 46.6 us -> none  [the longest x1 13.3 us: on_device(): lax.dot_general(masked, full_weight, (((1,), (1,)), ((), ())), preferred_...]
    pallas_call x0 -> x9, Pallas kernels: none -> 39.2 us  [the longest x1 15.7 us: down_grad(): pl.pallas_call(lambda *refs: down_kernel(per, blocks, rank, *refs), grid_...]
    ppermute x0 -> x19, starting transfers between devices: none -> 28 us  [swap(): return lax.ppermute(value, 'fsdp', [(i, i ^ mask) for i in range(devices)])]
    unnamed x11 -> x54, local copies, waits for them, and re-layouts: 22 us -> 3.6 us
    another operation x2 -> x0, local copies, waits for them, and re-layouts: 11 us -> none  [the longest x1 9.68 us: on_device(): grad_in_all = jnp.stack(grad_in_list, axis=0)]
    all_to_all x4 -> x2, starting transfers between devices: 21.7 us -> 12.3 us  [the longest x1 6.55 us: on_device(): lax.all_to_all(up_send, 'fsdp', split_axis=0, concat_axis=0, tiled=True)]
  transfers between devices with their start and end apart: 5 -> 21, of which waited for: 4 -> 7; matrix products, arithmetic and copies ran while one was open for 20% -> 1% of each run, Pallas kernels for 0% -> 17%
where the time goes in v1:
time: 201 us; the launch traced here: 199 us
  waiting for transfers between devices  111 us (55%)
  starting transfers between devices  40.2 us (20%)
  Pallas kernels  39.2 us (20%)
  local copies, waits for them, and re-layouts  6.05 us (3%)
    ppermute x19, waiting for transfers between devices, swap(): return lax.ppermute(value, 'fsdp', [(i, i ^ mask) for i in range(devices)])  79.7 us
    ppermute x19, starting transfers between devices, swap(): return lax.ppermute(value, 'fsdp', [(i, i ^ mask) for i in range(devices)])  28 us
    all_to_all x1, waiting for transfers between devices, on_device(): lax.all_to_all(eg_got, 'fsdp', split_axis=0, concat_axis=0, tiled=True)  26.9 us
    pallas_call x1, Pallas kernels, down_grad(): pl.pallas_call(lambda *refs: down_kernel(per, blocks, rank, *refs), grid_...  15.7 us
    pallas_call x1, Pallas kernels, main_parts(): pl.pallas_call(lambda *refs: main_kernel(outer, sub, kv, *refs), out_shap...  10.3 us
    all_to_all x1, starting transfers between devices, on_device(): lax.all_to_all(up_send, 'fsdp', split_axis=0, concat_axis=0, tiled=True)  6.55 us
    all_to_all x1, starting transfers between devices, on_device(): lax.all_to_all(eg_got, 'fsdp', split_axis=0, concat_axis=0, tiled=True)  5.72 us
    all_to_all x1, waiting for transfers between devices, on_device(): lax.all_to_all(up_send, 'fsdp', split_axis=0, concat_axis=0, tiled=True)  4.17 us
  transfers between devices with their start and end apart: 21, of which 7 were waited for; matrix products, arithmetic and copies ran while one was open for 1% of the time, Pallas kernels for 17%

profile of v1, /device:TPU:11, one launch (start us, length us, event | category | flops | bytes accessed | tf_op | source)
XLA Modules:
  0.0 198.6 jit_solution(11914193964738273948)
XLA Ops:
  1.9 1.3 gather_fusion
  3.1 6.6 %all-to-all-start = ((bf16[16,8,1024]{2,1,0:T(8,128)(2,1)}), bf16[16,8,1024]{2,1,0:T(8,128)(2,1)S(1)}, u32[]{:S(2)}, u32[]{:S(2)}) async-start(bf16[16,8,1024]{2,1,0:T(8,128)(2,1)} %gather_fusion), calls=%async_computation | async-start | bytes 524288 | tf_op jit(solution)/shard_map/all_to_all | solution.py:399
  9.7 3.7 %pick_factors.1 = (bf16[8,512,128]{2,1,0:T(8,128)(2,1)}, bf16[8,512,128]{2,1,0:T(8,128)(2,1)}) custom-call(s32[1]{0:T(128)} %bitcast.refs_0_, s32[16]{0:T(128)} %refs_0_, bf16[64,512,128]{2,1,0:T(8,128)(2,1)} %refs_2_.3), custom_call_target="tpu_custom_call" | custom-call | flops 1 | bytes 1 | tf_op jit(solution)/shard_map/pick_factors/pallas_call | solution.py:52
  13.5 4.2 %all-to-all-done = bf16[16,8,1024]{2,1,0:T(8,128)(2,1)S(1)} async-done(((bf16[16,8,1024]{2,1,0:T(8,128)(2,1)}), bf16[16,8,1024]{2,1,0:T(8,128)(2,1)S(1)}, u32[]{:S(2)}, u32[]{:S(2)}) %all-to-all-start) | async-done | bytes 262176 | tf_op jit(solution)/shard_map/all_to_all | solution.py:399
  17.7 1.0 collective-permute-start.4
  19.1 1.1 slice.14
  20.2 0.8 collective-permute-start.5
  21.7 0.9 copy-done.20
  22.7 0.8 first_sends.1
  25.6 16.8 %collective-permute-done.4.refs_2_.refs_7_ = bf16[8,512,128]{2,1,0:T(8,128)(2,1)S(1)} collective-permute-done((bf16[8,512,128]{2,1,0:T(8,128)(2,1)}, bf16[8,512,128]{2,1,0:T(8,128)(2,1)S(1)}, u32[]{:S(2)}, u32[]{:S(2)}) %collective-permute-start.4) | collective-permute-done | bytes 1048608 | tf_op jit(solution)/shard_map/ppermute | solution.py:383
  42.5 22.4 %collective-permute-done.1.refs_3_ = bf16[512,1024]{1,0:T(8,128)(2,1)S(1)} collective-permute-done((bf16[512,1024]{1,0:T(8,128)(2,1)}, bf16[512,1024]{1,0:T(8,128)(2,1)S(1)}, u32[]{:S(2)}, u32[]{:S(2)}) %collective-permute-start.1) | collective-permute-done | bytes 1048608 | tf_op jit(solution)/shard_map/ppermute | solution.py:383
  64.9 1.0 collective-permute-start.6
  66.1 12.8 %collective-permute-start.2 = (bf16[256,1024]{1,0:T(8,128)(2,1)S(1)}, bf16[256,1024]{1,0:T(8,128)(2,1)S(1)}, u32[]{:S(2)}, u32[]{:S(2)}) collective-permute-start(bf16[256,1024]{1,0:T(8,128)(2,1)S(1)} %get-tuple-element.91), channel_id=1, source_target_pairs={{0,1},{1,0},{2,3},{3,2},{4,5},{5,4},{6,7},{7,6},{8,9},{9,8},{10,11... | collective-permute-start | bytes 1572872 | tf_op jit(solution)/shard_map/ppermute | solution.py:383
  78.9 18.2 %collective-permute-done.9.refs_8_.refs_13_.refs_4_ = bf16[128,3200]{1,0:T(8,128)(2,1)S(1)} collective-permute-done((bf16[128,3200]{1,0:T(8,128)(2,1)S(1)}, bf16[128,3200]{1,0:T(8,128)(2,1)S(1)}, u32[]{:S(2)}, u32[]{:S(2)}) %collective-permute-start.9) | collective-permute-done | bytes 819232 | tf_op jit(solution)/shard_map/ppermute | solution.py:383
  98.0 1.8 collective-permute-start.11
  99.7 0.9 collective-permute-start.12
  100.7 10.3 %plane_products.1 = (bf16[128,2048]{1,0:T(8,128)(2,1)S(1)}, f32[128,1024]{1,0:T(8,128)S(1)}, bf16[128,3072]{1,0:T(8,128)(2,1)}, bf16[128,3072]{1,0:T(8,128)(2,1)}, bf16[128,3072]{1,0:T(8,128)(2,1)}) custom-call(s32[1]{0:T(128)} %bitcast.refs_0_, bf16[512,1024]{1,0:T(8,128)(2,1)} %refs_1_.6, bf16[512,1024]{1,0:T(8,128)(2,1)} %copy-done.26, ...), custom_call_target="tpu_custom_call" | custom-call | flops 1 | bytes 1 | tf_op jit(solution)/shard_map/plane_products/pallas_call | solution.py:163
  111.0 0.8 shrunk_rows.1
  111.9 1.3 pack_columns.1
  113.2 1.9 collective-permute-start.16
  115.8 1.2 collective-permute-start.14
  117.8 1.1 collective-permute-start.17
  118.9 0.8 copy-done.12
  119.8 1.4 collective-permute-start.18
  121.2 5.7 %all-to-all-start.1 = ((bf16[16,8,1024]{2,1,0:T(8,128)(2,1)}), bf16[16,8,1024]{2,1,0:T(8,128)(2,1)S(1)}, u32[]{:S(2)}, u32[]{:S(2)}) async-start(bf16[16,8,1024]{2,1,0:T(8,128)(2,1)} %bitcast.5), calls=%async_computation.1 | async-start | bytes 524288 | tf_op jit(solution)/shard_map/all_to_all | solution.py:425
  126.9 6.5 %collective-permute-done.17.refs_4_ = bf16[512,640]{1,0:T(8,128)(2,1)} collective-permute-done((bf16[512,640]{1,0:T(8,128)(2,1)}, bf16[512,640]{1,0:T(8,128)(2,1)}, u32[]{:S(2)}, u32[]{:S(2)}) %collective-permute-start.17) | collective-permute-done | bytes 655392 | tf_op jit(solution)/shard_map/ppermute | solution.py:383
  133.5 15.7 %collective-permute-done.18.refs_5_ = bf16[512,640]{1,0:T(8,128)(2,1)} collective-permute-done((bf16[512,640]{1,0:T(8,128)(2,1)}, bf16[512,640]{1,0:T(8,128)(2,1)}, u32[]{:S(2)}, u32[]{:S(2)}) %collective-permute-start.18) | collective-permute-done | bytes 655392 | tf_op jit(solution)/shard_map/ppermute | solution.py:383
  149.2 1.1 copy-done.13
  150.3 15.7 %down_gradient.1 = f32[64,512,128]{2,1,0:T(8,128)} custom-call(s32[1]{0:T(128)} %bitcast.refs_0_, s32[16]{0:T(128)S(1)} %copy-done.22, bf16[512,640]{1,0:T(8,128)(2,1)S(1)} %get-tuple-element.80.refs_2_, bf16[512,640]{1,0:T(8,128)(2,1)S(1)} %copy-done.13, bf16[512,640]{1,0:T(8,128)(2,1)} %collective-permute-done.17.refs_4_, ...), custom_call_target="tpu_custom_call" | custom-call | flops 1 | bytes 1 | tf_op jit(solution)/shard_map/down_gradient/pallas_call | solution.py:303
  166.0 26.9 %all-to-all-done.1.refs_1_ = bf16[16,8,1024]{2,1,0:T(8,128)(2,1)S(1)} async-done(((bf16[16,8,1024]{2,1,0:T(8,128)(2,1)}), bf16[16,8,1024]{2,1,0:T(8,128)(2,1)S(1)}, u32[]{:S(2)}, u32[]{:S(2)}) %all-to-all-start.1) | async-done | bytes 262176 | tf_op jit(solution)/shard_map/all_to_all | solution.py:425
  192.9 3.0 %up_gradient.1 = f32[64,8,1024]{2,1,0:T(8,128)} custom-call(s32[16]{0:T(128)S(1)} %copy-done.22, bf16[16,8,1024]{2,1,0:T(8,128)(2,1)S(1)} %all-to-all-done.1.refs_1_), custom_call_target="tpu_custom_call" | custom-call | flops 1 | bytes 1 | tf_op jit(solution)/shard_map/up_gradient/pallas_call | solution.py:337
  195.9 2.7 %join_columns.1 = (bf16[128,1024]{1,0:T(8,128)(2,1)}, bf16[128,8192]{1,0:T(8,128)(2,1)}) custom-call(s32[1]{0:T(128)} %bitcast.refs_0_, bf16[128,2048]{1,0:T(8,128)(2,1)S(1)} %copy-done.15, f32[128,1024]{1,0:T(8,128)S(1)} %copy-done.17, f32[128,1024]{1,0:T(8,128)S(1)} %copy-done.19, bf16[128,3072]{1,0:T(8,128)(2,1)S(1)} %collective-permute-done.13.refs_4_, ...), custom_call_target="tpu_custom_call" | custom-call | flops 1 | bytes 1 | tf_op jit(solution)/shard_map/join_columns/pallas_call | solution.py:365
  (78 shorter events, 6.3 us)
Async XLA Ops:
  3.1 14.5 %all-to-all-start = ((bf16[16,8,1024]{2,1,0:T(8,128)(2,1)}), bf16[16,8,1024]{2,1,0:T(8,128)(2,1)S(1)}, u32[]{:S(2)}, u32[]{:S(2)}) async-start(bf16[16,8,1024]{2,1,0:T(8,128)(2,1)} %gather_fusion), calls=%async_computation | async-start | bytes 524288 | tf_op jit(solution)/shard_map/all_to_all | solution.py:399
  9.7 12.0 %copy-start.11 = (bf16[128,8192]{1,0:T(8,128)(2,1)S(1)}, bf16[128,8192]{1,0:T(8,128)(2,1)}, u32[]{:S(2)}) copy-start(bf16[128,8192]{1,0:T(8,128)(2,1)} %refs_4_.1) | copy-start | bytes 6291460
  9.7 12.0 %copy-start.22 = (s32[16]{0:T(128)S(1)}, s32[16]{0:T(128)}, u32[]{:S(2)}) copy-start(s32[16]{0:T(128)} %refs_0_) | copy-start | bytes 196
  9.7 12.0 %copy-start.23 = (s32[64]{0:T(128)S(1)}, s32[64]{0:T(128)}, u32[]{:S(2)}) copy-start(s32[64]{0:T(128)} %refs_2_.5) | copy-start | bytes 772
  17.7 24.8 %collective-permute-start.4 = (bf16[8,512,128]{2,1,0:T(8,128)(2,1)}, bf16[8,512,128]{2,1,0:T(8,128)(2,1)S(1)}, u32[]{:S(2)}, u32[]{:S(2)}) collective-permute-start(bf16[8,512,128]{2,1,0:T(8,128)(2,1)} %get-tuple-element.51), channel_id=1, source_target_pairs={{0,2},{1,3},{2,0},{3,1},{4,6},{5,7},{6,4},{7,5},{8,10},{9,11},{10,... | collective-permute-start | bytes 3145736 | tf_op jit(solution)/shard_map/ppermute | solution.py:383
  18.7 46.2 %collective-permute-start.1 = (bf16[512,1024]{1,0:T(8,128)(2,1)}, bf16[512,1024]{1,0:T(8,128)(2,1)S(1)}, u32[]{:S(2)}, u32[]{:S(2)}) collective-permute-start(bf16[512,1024]{1,0:T(8,128)(2,1)} %refs_1_.6), channel_id=1, source_target_pairs={{0,2},{1,3},{2,0},{3,1},{4,6},{5,7},{6,4},{7,5},{8,10},{9,11},{10,... | collective-permute-start | bytes 3145736 | tf_op jit(solution)/shard_map/ppermute | solution.py:383
  20.2 4.8 %collective-permute-start.5 = (bf16[4,512,128]{2,1,0:T(8,128)(2,1)S(1)}, bf16[4,512,128]{2,1,0:T(8,128)(2,1)S(1)}, u32[]{:S(2)}, u32[]{:S(2)}) collective-permute-start(bf16[4,512,128]{2,1,0:T(8,128)(2,1)S(1)} %slice.14), channel_id=1, source_target_pairs={{0,1},{1,0},{2,3},{3,2},{4,5},{5,4},{6,7},{7,6},{8,9},{9,8},{10,11... | collective-permute-start | bytes 1572872 | tf_op jit(solution)/shard_map/ppermute | solution.py:383
  23.5 74.3 %copy-start.1 = (bf16[128,3200]{1,0:T(8,128)(2,1)}, bf16[128,3200]{1,0:T(8,128)(2,1)S(1)}, u32[]{:S(2)}) copy-start(bf16[128,3200]{1,0:T(8,128)(2,1)S(1)} %get-tuple-element.76.refs_5_.refs_10_.refs_8_.refs_1_) | copy-start | bytes 2457604
  23.5 73.5 %copy-start.9 = (bf16[8,512,128]{2,1,0:T(8,128)(2,1)S(1)}, bf16[8,512,128]{2,1,0:T(8,128)(2,1)}, u32[]{:S(2)}) copy-start(bf16[8,512,128]{2,1,0:T(8,128)(2,1)} %get-tuple-element.49.refs_1_.refs_6_) | copy-start | bytes 3145732
  23.5 42.4 %collective-permute-start.7 = (bf16[128,3200]{1,0:T(8,128)(2,1)S(1)}, bf16[128,3200]{1,0:T(8,128)(2,1)S(1)}, u32[]{:S(2)}, u32[]{:S(2)}) collective-permute-start(bf16[128,3200]{1,0:T(8,128)(2,1)S(1)} %get-tuple-element.54), channel_id=1, source_target_pairs={{0,4},{1,5},{2,6},{3,7},{4,0},{5,1},{6,2},{7,3},{8,12},{9,13},{10,... | collective-permute-start | bytes 2457608 | tf_op jit(solution)/shard_map/ppermute | solution.py:383
  24.2 41.8 %collective-permute-start.8 = (bf16[128,3200]{1,0:T(8,128)(2,1)S(1)}, bf16[128,3200]{1,0:T(8,128)(2,1)S(1)}, u32[]{:S(2)}, u32[]{:S(2)}) collective-permute-start(bf16[128,3200]{1,0:T(8,128)(2,1)S(1)} %get-tuple-element.55), channel_id=1, source_target_pairs={{0,8},{1,9},{2,10},{3,11},{4,12},{5,13},{6,14},{7,15},{8,0},{9,1},... | collective-permute-start | bytes 2457608 | tf_op jit(solution)/shard_map/ppermute | solution.py:383
  25.0 74.7 %collective-permute-start = (bf16[512,1024]{1,0:T(8,128)(2,1)S(1)}, bf16[512,1024]{1,0:T(8,128)(2,1)S(1)}, u32[]{:S(2)}, u32[]{:S(2)}) collective-permute-start(bf16[512,1024]{1,0:T(8,128)(2,1)S(1)} %copy-done.25), channel_id=1, source_target_pairs={{0,1},{1,0},{2,3},{3,2},{4,5},{5,4},{6,7},{7,6},{8,9},{9,8},{10,11... | collective-permute-start | bytes 3145736 | tf_op jit(solution)/shard_map/ppermute | solution.py:383
  42.4 55.4 %copy-start.10 = (bf16[8,512,128]{2,1,0:T(8,128)(2,1)}, bf16[8,512,128]{2,1,0:T(8,128)(2,1)S(1)}, u32[]{:S(2)}) copy-start(bf16[8,512,128]{2,1,0:T(8,128)(2,1)S(1)} %collective-permute-done.4.refs_2_.refs_7_) | copy-start | bytes 3145732
  42.4 54.6 %collective-permute-start.9 = (bf16[128,3200]{1,0:T(8,128)(2,1)S(1)}, bf16[128,3200]{1,0:T(8,128)(2,1)S(1)}, u32[]{:S(2)}, u32[]{:S(2)}) collective-permute-start(bf16[128,3200]{1,0:T(8,128)(2,1)S(1)} %get-tuple-element.56), channel_id=1, source_target_pairs={{0,12},{1,13},{2,14},{3,15},{4,8},{5,9},{6,10},{7,11},{8,4},{9,5},... | collective-permute-start | bytes 2457608 | tf_op jit(solution)/shard_map/ppermute | solution.py:383
  64.9 32.9 %copy-start.24 = (bf16[512,1024]{1,0:T(8,128)(2,1)}, bf16[512,1024]{1,0:T(8,128)(2,1)S(1)}, u32[]{:S(2)}) copy-start(bf16[512,1024]{1,0:T(8,128)(2,1)S(1)} %collective-permute-done.1.refs_3_) | copy-start | bytes 3145732
  64.9 32.2 %collective-permute-start.6 = (bf16[4,512,128]{2,1,0:T(8,128)(2,1)S(1)}, bf16[4,512,128]{2,1,0:T(8,128)(2,1)S(1)}, u32[]{:S(2)}, u32[]{:S(2)}) collective-permute-start(bf16[4,512,128]{2,1,0:T(8,128)(2,1)S(1)} %slice.20), channel_id=1, source_target_pairs={{0,1},{1,0},{2,3},{3,2},{4,5},{5,4},{6,7},{7,6},{8,9},{9,8},{10,11... | collective-permute-start | bytes 1572872 | tf_op jit(solution)/shard_map/ppermute | solution.py:383
  66.0 31.8 %copy-start.3 = (bf16[128,3200]{1,0:T(8,128)(2,1)}, bf16[128,3200]{1,0:T(8,128)(2,1)S(1)}, u32[]{:S(2)}) copy-start(bf16[128,3200]{1,0:T(8,128)(2,1)S(1)} %collective-permute-done.7.refs_6_.refs_11_.refs_2_) | copy-start | bytes 2457604
  66.0 34.6 %collective-permute-start.3 = (bf16[256,1024]{1,0:T(8,128)(2,1)S(1)}, bf16[256,1024]{1,0:T(8,128)(2,1)S(1)}, u32[]{:S(2)}, u32[]{:S(2)}) collective-permute-start(bf16[256,1024]{1,0:T(8,128)(2,1)S(1)} %get-tuple-element.90), channel_id=1, source_target_pairs={{0,1},{1,0},{2,3},{3,2},{4,5},{5,4},{6,7},{7,6},{8,9},{9,8},{10,11... | collective-permute-start | bytes 1572872 | tf_op jit(solution)/shard_map/ppermute | solution.py:383
  66.1 31.7 %copy-start.5 = (bf16[128,3200]{1,0:T(8,128)(2,1)}, bf16[128,3200]{1,0:T(8,128)(2,1)S(1)}, u32[]{:S(2)}) copy-start(bf16[128,3200]{1,0:T(8,128)(2,1)S(1)} %collective-permute-done.8.refs_7_.refs_12_.refs_3_) | copy-start | bytes 2457604
  66.1 34.5 %collective-permute-start.2 = (bf16[256,1024]{1,0:T(8,128)(2,1)S(1)}, bf16[256,1024]{1,0:T(8,128)(2,1)S(1)}, u32[]{:S(2)}, u32[]{:S(2)}) collective-permute-start(bf16[256,1024]{1,0:T(8,128)(2,1)S(1)} %get-tuple-element.91), channel_id=1, source_target_pairs={{0,1},{1,0},{2,3},{3,2},{4,5},{5,4},{6,7},{7,6},{8,9},{9,8},{10,11... | collective-permute-start | bytes 1572872 | tf_op jit(solution)/shard_map/ppermute | solution.py:383
  98.0 13.0 %collective-permute-start.10 = (f32[128,128]{1,0:T(8,128)S(1)}, f32[128,128]{1,0:T(8,128)S(1)}, u32[]{:S(2)}, u32[]{:S(2)}) collective-permute-start(f32[128,128]{1,0:T(8,128)S(1)} %get-tuple-element.58), channel_id=1, source_target_pairs={{0,4},{1,5},{2,6},{3,7},{4,0},{5,1},{6,2},{7,3},{8,12},{9,13},{10,... | collective-permute-start | bytes 196616 | tf_op jit(solution)/shard_map/ppermute | solution.py:383
  98.0 13.0 %collective-permute-start.11 = (f32[128,128]{1,0:T(8,128)S(1)}, f32[128,128]{1,0:T(8,128)S(1)}, u32[]{:S(2)}, u32[]{:S(2)}) collective-permute-start(f32[128,128]{1,0:T(8,128)S(1)} %get-tuple-element.59), channel_id=1, source_target_pairs={{0,8},{1,9},{2,10},{3,11},{4,12},{5,13},{6,14},{7,15},{8,0},{9,1},... | collective-permute-start | bytes 196616 | tf_op jit(solution)/shard_map/ppermute | solution.py:383
  99.7 11.3 %collective-permute-start.12 = (f32[128,128]{1,0:T(8,128)S(1)}, f32[128,128]{1,0:T(8,128)S(1)}, u32[]{:S(2)}, u32[]{:S(2)}) collective-permute-start(f32[128,128]{1,0:T(8,128)S(1)} %get-tuple-element.60), channel_id=1, source_target_pairs={{0,12},{1,13},{2,14},{3,15},{4,8},{5,9},{6,10},{7,11},{8,4},{9,5},... | collective-permute-start | bytes 196616 | tf_op jit(solution)/shard_map/ppermute | solution.py:383
  100.6 11.3 %copy-start.8 = (bf16[128,3200]{1,0:T(8,128)(2,1)S(1)}, bf16[128,3200]{1,0:T(8,128)(2,1)}, u32[]{:S(2)}) copy-start(bf16[128,3200]{1,0:T(8,128)(2,1)} %copy-done.7) | copy-start | bytes 2457604
  113.2 5.7 %collective-permute-start.16 = (bf16[512,640]{1,0:T(8,128)(2,1)S(1)}, bf16[512,640]{1,0:T(8,128)(2,1)S(1)}, u32[]{:S(2)}, u32[]{:S(2)}) collective-permute-start(bf16[512,640]{1,0:T(8,128)(2,1)S(1)} %get-tuple-element.81), channel_id=1, source_target_pairs={{0,1},{1,0},{2,3},{3,2},{4,5},{5,4},{6,7},{7,6},{8,9},{9,8},{10,11... | collective-permute-start | bytes 1966088 | tf_op jit(solution)/shard_map/ppermute | solution.py:383
  115.2 80.7 %collective-permute-start.13 = (bf16[128,3072]{1,0:T(8,128)(2,1)}, bf16[128,3072]{1,0:T(8,128)(2,1)S(1)}, u32[]{:S(2)}, u32[]{:S(2)}) collective-permute-start(bf16[128,3072]{1,0:T(8,128)(2,1)} %get-tuple-element.67), channel_id=1, source_target_pairs={{0,4},{1,5},{2,6},{3,7},{4,0},{5,1},{6,2},{7,3},{8,12},{9,13},{10,... | collective-permute-start | bytes 2359304 | tf_op jit(solution)/shard_map/ppermute | solution.py:383
  115.8 80.1 %collective-permute-start.14 = (bf16[128,3072]{1,0:T(8,128)(2,1)}, bf16[128,3072]{1,0:T(8,128)(2,1)S(1)}, u32[]{:S(2)}, u32[]{:S(2)}) collective-permute-start(bf16[128,3072]{1,0:T(8,128)(2,1)} %get-tuple-element.68), channel_id=1, source_target_pairs={{0,8},{1,9},{2,10},{3,11},{4,12},{5,13},{6,14},{7,15},{8,0},{9,1},... | collective-permute-start | bytes 2359304 | tf_op jit(solution)/shard_map/ppermute | solution.py:383
  117.0 78.8 %collective-permute-start.15 = (bf16[128,3072]{1,0:T(8,128)(2,1)}, bf16[128,3072]{1,0:T(8,128)(2,1)}, u32[]{:S(2)}, u32[]{:S(2)}) collective-permute-start(bf16[128,3072]{1,0:T(8,128)(2,1)} %get-tuple-element.69), channel_id=1, source_target_pairs={{0,12},{1,13},{2,14},{3,15},{4,8},{5,9},{6,10},{7,11},{8,4},{9,5},... | collective-permute-start | bytes 2359304 | tf_op jit(solution)/shard_map/ppermute | solution.py:383
  117.8 15.6 %collective-permute-start.17 = (bf16[512,640]{1,0:T(8,128)(2,1)}, bf16[512,640]{1,0:T(8,128)(2,1)}, u32[]{:S(2)}, u32[]{:S(2)}) collective-permute-start(bf16[512,640]{1,0:T(8,128)(2,1)} %get-tuple-element.82), channel_id=1, source_target_pairs={{0,2},{1,3},{2,0},{3,1},{4,6},{5,7},{6,4},{7,5},{8,10},{9,11},{10,... | collective-permute-start | bytes 1966088 | tf_op jit(solution)/shard_map/ppermute | solution.py:383
  119.8 29.4 %collective-permute-start.18 = (bf16[512,640]{1,0:T(8,128)(2,1)}, bf16[512,640]{1,0:T(8,128)(2,1)}, u32[]{:S(2)}, u32[]{:S(2)}) collective-permute-start(bf16[512,640]{1,0:T(8,128)(2,1)} %get-tuple-element.83), channel_id=1, source_target_pairs={{0,3},{1,2},{2,1},{3,0},{4,7},{5,6},{6,5},{7,4},{8,11},{9,10},{10,... | collective-permute-start | bytes 1966088 | tf_op jit(solution)/shard_map/ppermute | solution.py:383
  121.2 71.7 %all-to-all-start.1 = ((bf16[16,8,1024]{2,1,0:T(8,128)(2,1)}), bf16[16,8,1024]{2,1,0:T(8,128)(2,1)S(1)}, u32[]{:S(2)}, u32[]{:S(2)}) async-start(bf16[16,8,1024]{2,1,0:T(8,128)(2,1)} %bitcast.5), calls=%async_computation.1 | async-start | bytes 524288 | tf_op jit(solution)/shard_map/all_to_all | solution.py:425
  166.0 29.9 %copy-start.15 = (bf16[128,2048]{1,0:T(8,128)(2,1)S(1)}, bf16[128,2048]{1,0:T(8,128)(2,1)}, u32[]{:S(2)}) copy-start(bf16[128,2048]{1,0:T(8,128)(2,1)} %copy-done.14) | copy-start | bytes 1572868
  (16 other events, 73.4 us)

commit v2 on v1

--- a/solution.py
+++ b/solution.py
@@ -61,35 +61,60 @@
     )(me, ids, factor)
 
 
-def first_kernel(outer, me_ref, ids_ref, ranks_ref, rows_ref, tokens, grad, up_ref, *outs):
+def mask_kernel(rows_ref, grad, out):
+    rows = lax.broadcasted_iota(jnp.int32, grad.shape, 0)
+    out[...] = jnp.where(rows < rows_ref[0], grad[...].astype(F32), 0.0).astype(BF)
+
+
+def mask_rows(block_rows, grad):
+    return pl.pallas_call(
+        mask_kernel,
+        out_shape=jax.ShapeDtypeStruct(grad.shape, BF),
+        in_specs=[SM, VM],
+        out_specs=VM,
+        compiler_params=params(8),
+        cost_estimate=COST,
+        name="mask_rows",
+    )(block_rows, grad)
+
+
+def first_kernel(outer, me_ref, ids_ref, ranks_ref, tokens, up_ref, *refs):
+    grads, outs = refs[:-outer], refs[-outer:]
     rank = ranks_ref[ids_ref[me_ref[0]]]
     plane = lax.div(me_ref[0], INNER)
     dz = tokens.shape[1] // outer
-    kv = grad.shape[1]
-    rows = lax.broadcasted_iota(jnp.int32, grad.shape, 0)
-    masked = jnp.where(rows < rows_ref[0], grad[...].astype(F32), 0.0).astype(BF)
-    back = dot(masked, up_ref[...], 1, 1) * adapter_scale(rank)
+    rank_cap, kv = up_ref.shape
+    back = dot(grads[0][...], up_ref[...], 1, 1) * adapter_scale(rank)
     cols = lax.broadcasted_iota(jnp.int32, back.shape, 1)
     back = jnp.where(cols < rank, back, 0.0).astype(BF)
     for k, out in enumerate(outs):
         at = pl.multiple_of(jnp.bitwise_xor(plane, k) * dz, dz)
         out[:, :dz] = tokens[:, pl.ds(at, dz)]
-        out[:, dz : dz + kv] = masked
-        out[:, dz + kv :] = back
-
-
-def first_sends(me, ids, ranks, block_rows, tokens, grad, up, outer):
+        out[:, dz : dz + rank_cap] = back
+    at = dz + rank_cap
+    for g in grads:
+        for row in range(0, g.shape[0], BLOCK):
+            outs[1][:, at : at + kv] = g[row : row + BLOCK, :]
+            at += kv
+
+
+def first_sends(me, ids, ranks, tokens, up, grads, outer):
     rows, width = tokens.shape
-    wide = width // outer + grad.shape[1] + up.shape[0]
+    rank_cap, kv = up.shape
+    wide = width // outer + rank_cap
+    more = outer // 2 * kv
     return pl.pallas_call(
         lambda *refs: first_kernel(outer, *refs),
-        out_shape=tuple(jax.ShapeDtypeStruct((rows, wide), BF) for _ in range(outer)),
-        in_specs=[SM] * 4 + [VM] * 3,
+        out_shape=tuple(
+            jax.ShapeDtypeStruct((rows, wide + (more if k == 1 else 0)), BF)
+            for k in range(outer)
+        ),
+        in_specs=[SM] * 3 + [VM] * (2 + len(grads)),
         out_specs=(VM,) * outer,
-        compiler_params=params(24),
+        compiler_params=params(32),
         cost_estimate=COST,
         name="first_sends",
-    )(me, ids, ranks, block_rows, tokens, grad, up)
+    )(me, ids, ranks, tokens, up, *grads)
 
 
 def plane_parts(me, w, s, scratch, outer, sub):
@@ -125,22 +150,36 @@
     return [pltpu.VMEM((dz, kv), BF), pltpu.VMEM((outer, dz, rank), BF)]
 
 
-def main_kernel(outer, sub, kv, me_ref, *refs):
+def main_kernel(evens, outer, sub, kv, me_ref, *refs):
     w = [[refs[0]], [refs[1]], [refs[2]], [refs[3], refs[4]]]
     s = [(refs[5], 0), (refs[7], 0), (refs[6], 0), (refs[8], 0)]
-    xe = refs[9 : 9 + outer]
-    held_t, held_f = refs[9 + outer : 11 + outer]
-    sends = refs[11 + outer : 10 + 2 * outer]
-    x, e, *scratch = refs[10 + 2 * outer :]
+    rank = refs[5].shape[2]
+    *ins, x, e = refs[9 : len(refs) - (0 if sub % 256 == 0 else 2)]
+    scratch = refs[9 + len(ins) + 2 :]
+    n_outs = 1 + outer + outer // 2
+    ins, outs = ins[:-n_outs], ins[-n_outs:]
+    held_t, *sends = outs[:outer]
+    held_f = outs[outer]
+    even_f = outs[outer + 1 : outer + outer // 2]
+    odd_f = outs[outer + outer // 2 :]
+    xe, grads = ins[:outer], ins[outer:]
     dz = sub * INNER
     for k in range(outer):
         x[k * BLOCK : (k + 1) * BLOCK, :] = xe[k][:, :dz]
-        e[k * BLOCK : (k + 1) * BLOCK, :] = xe[k][:, dz : dz + kv]
+    at = 0
+    for g in grads:
+        for row in range(0, g.shape[0], BLOCK):
+            k = evens[at]
+            e[k * BLOCK : (k + 1) * BLOCK, :] = g[row : row + BLOCK, :]
+            first = dz + rank + at * kv
+            k = k ^ 1
+            e[k * BLOCK : (k + 1) * BLOCK, :] = xe[1][:, first : first + kv]
+            at += 1
     parts = plane_parts(me_ref[0], w, s, scratch, outer, sub)
     for first, size, weight, factors in parts:
         base = dot(e[...], weight[...], 1, 1)
         for k in range(outer):
-            extra = dot(xe[k][:, dz + kv :], factors[k][...], 1, 1)
+            extra = dot(xe[k][:, dz : dz + rank], factors[k][...], 1, 1)
             out = held_t if k == 0 else sends[k - 1]
             rows = slice(k * BLOCK, (k + 1) * BLOCK)
             out[:, pl.ds(first, size)] = (base[rows] + extra).astype(BF)
@@ -150,25 +189,36 @@
             dot(x[:, pl.ds(first, size)], weight[:, c : c + step], 1, 0)
             for first, size, weight, _ in parts
         )
-        held_f[:, c : c + step] = part[:BLOCK]
-        for k in range(1, outer):
-            rows = slice(k * BLOCK, (k + 1) * BLOCK)
-            sends[k - 1][:, dz + c : dz + c + step] = part[rows].astype(BF)
-
-
-def main_parts(me, wparts, sparts, xe, outer):
+        for k in range(outer):
+            value = part[k * BLOCK : (k + 1) * BLOCK]
+            cols = slice(c, c + step)
+            if k == 0:
+                held_f[:, cols] = value
+            elif k == 1:
+                sends[0][:, dz + c : dz + c + step] = value.astype(BF)
+            elif k % 2 == 0:
+                even_f[k // 2 - 1][:, cols] = value
+            else:
+                row = (k // 2 - 1) * BLOCK
+                odd_f[0][row : row + BLOCK, cols] = value.astype(BF)
+
+
+def main_parts(me, wparts, sparts, xe, grads, evens, outer):
     sub, kv = wparts[0].shape
     rank = sparts[0].shape[-1]
     dz = sub * INNER
-    return pl.pallas_call(
-        lambda *refs: main_kernel(outer, sub, kv, *refs),
+    half = outer // 2
+    return pl.pallas_call(
+        lambda *refs: main_kernel(evens, outer, sub, kv, *refs),
         out_shape=(
             jax.ShapeDtypeStruct((BLOCK, dz), BF),
-            jax.ShapeDtypeStruct((BLOCK, kv), F32),
+            jax.ShapeDtypeStruct((BLOCK, dz + kv), BF),
         )
-        + tuple(jax.ShapeDtypeStruct((BLOCK, dz + kv), BF) for _ in range(outer - 1)),
-        in_specs=[SM] + [VM] * (9 + outer),
-        out_specs=(VM,) * (1 + outer),
+        + (jax.ShapeDtypeStruct((BLOCK, dz), BF),) * (outer - 2)
+        + (jax.ShapeDtypeStruct((BLOCK, kv), F32),) * half
+        + (jax.ShapeDtypeStruct(((half - 1) * BLOCK, kv), BF),),
+        in_specs=[SM] + [VM] * (9 + outer + len(grads)),
+        out_specs=(VM,) * (1 + outer + half),
         scratch_shapes=[
             pltpu.VMEM((outer * BLOCK, dz), BF),
             pltpu.VMEM((outer * BLOCK, kv), BF),
@@ -177,7 +227,7 @@
         compiler_params=params(48),
         cost_estimate=COST,
         name="plane_products",
-    )(me, *wparts, *sparts, *xe)
+    )(me, *wparts, *sparts, *xe, *grads)
 
 
 def shrink_kernel(outer, sub, me_ref, *refs):
@@ -215,7 +265,7 @@
     )(me, *sparts, *xe)
 
 
-def rows_kernel(outer, dz, me_ref, ids_ref, ranks_ref, *refs):
+def rows_kernel(outer, me_ref, ids_ref, ranks_ref, *refs):
     parts = refs[:outer]
     up, own, extra, eg = refs[outer:]
     rank = ranks_ref[ids_ref[me_ref[0]]]
@@ -224,15 +274,14 @@
     shrink = jnp.where(cols < rank, low, 0.0).astype(BF)
     scale = adapter_scale(rank)[:, :1]
     extra[...] = dot(shrink, up[...], 1, 0) * scale
-    kv = up.shape[1]
-    eg[...] = (dot(shrink, own[:, dz : dz + kv], 0, 0) * scale).astype(BF)
+    eg[...] = (dot(shrink, own[...], 0, 0) * scale).astype(BF)
 
 
 def shrunk_rows(me, ids, ranks, parts, up, own):
     rank_cap, kv = up.shape
     outer = len(parts)
     return pl.pallas_call(
-        lambda *refs: rows_kernel(outer, own.shape[1] - kv - rank_cap, *refs),
+        lambda *refs: rows_kernel(outer, *refs),
         out_shape=(
             jax.ShapeDtypeStruct((BLOCK, kv), F32),
             jax.ShapeDtypeStruct((rank_cap, kv), BF),
@@ -248,10 +297,10 @@
 def pack_kernel(outer, sub, rank, me_ref, *refs):
     xe, outs = refs[:outer], refs[outer:]
     own = lax.rem(me_ref[0], INNER)
-    last = xe[0].shape[1] - rank
+    last = sub * INNER
     for j, out in enumerate(outs):
         for k in range(outer):
-            out[k * BLOCK : (k + 1) * BLOCK, :rank] = xe[k][:, last:]
+            out[k * BLOCK : (k + 1) * BLOCK, :rank] = xe[k][:, last : last + rank]
         for quarter in range(INNER):
 
             @pl.when(jnp.bitwise_xor(own, j) == quarter)
@@ -350,16 +399,16 @@
 
 
 def join_kernel(outer, dz, me_ref, held_t, held_f, extra, *refs):
-    got, proj, grad = refs[:-2], refs[-2], refs[-1]
+    got, parts, (proj, grad) = refs[: outer - 1], refs[outer - 1 : -2], refs[-2:]
     plane = lax.div(me_ref[0], INNER)
     for k in range(outer):
         at = pl.multiple_of(jnp.bitwise_xor(plane, k) * dz, dz)
         grad[:, pl.ds(at, dz)] = held_t[...] if k == 0 else got[k - 1][:, :dz]
-    total = held_f[...] + extra[...] + sum(g[:, dz:].astype(F32) for g in got)
-    proj[...] = total.astype(BF)
-
-
-def join(me, held_t, held_f, extra, got):
+    total = held_f[...] + extra[...] + got[0][:, dz:].astype(F32)
+    proj[...] = (total + sum(p[...].astype(F32) for p in parts)).astype(BF)
+
+
+def join(me, held_t, held_f, extra, got, parts):
     rows, dz = held_t.shape
     outer = 1 + len(got)
     return pl.pallas_call(
@@ -368,12 +417,12 @@
             jax.ShapeDtypeStruct(held_f.shape, BF),
             jax.ShapeDtypeStruct((rows, dz * outer), BF),
         ),
-        in_specs=[SM] + [VM] * (2 + outer),
+        in_specs=[SM] + [VM] * (2 + outer + len(parts)),
         out_specs=(VM, VM),
         compiler_params=params(24),
         cost_estimate=COST,
         name="join_columns",
-    )(me, held_t, held_f, extra, *got)
+    )(me, held_t, held_f, extra, *got, *parts)
 
 
 def build(devices):
@@ -392,34 +441,47 @@
             return lax.optimization_barrier((value, earlier))[0]
 
         def to_planes(parts):
-            got = {k: swap(parts[k], k * INNER) for k in reversed(range(1, outer))}
+            got = {k: swap(parts[k], k * INNER) for k in range(1, outer)}
             return [parts[0]] + [got[k] for k in range(1, outer)]
 
-        up_send = jnp.take(expand_factor, block_adapter, axis=0, mode="clip")
+        masked = mask_rows(block_rows, grad_out)
+        grads, evens = [masked], [0]
+        step = outer // 2
+        while step > 1:
+            stack = grads[0] if len(grads) == 1 else jnp.concatenate(grads, axis=0)
+            grads.append(swap(stack, step * INNER))
+            evens = evens + [k ^ step for k in evens]
+            step //= 2
+
+        up_send = jnp.take(expand_factor, after(block_adapter, masked), axis=0, mode="clip")
         up = lax.all_to_all(up_send, "fsdp", split_axis=0, concat_axis=0, tiled=True)
         up = up.reshape(rank, kv)
 
         s_send, s_keep = pick(me, after(block_adapter, up_send), shrink_factor, outer)
-        s_x = swap(after(s_send, up), 2)
-        w_x = swap(after(base_weight, up), 2)
-        s_c = swap(s_keep[outer:], 1)
+        s_x = swap(after(s_send, (up, grads)), 2)
+        w_x = swap(after(base_weight, (up, grads, s_keep)), 2)
+        s_c = swap(after(s_keep, s_x)[outer:], 1)
         s_xc = swap(s_x[outer:], 1)
-        w_c = swap(base_weight, 1)
+        w_c = swap(after(base_weight, w_x), 1)
         w_xc = [swap(w_x[: sub // 2], 1), swap(w_x[sub // 2 :], 1)]
         wparts = (base_weight, w_c, w_x, *w_xc)
         sparts = (s_keep, s_x, s_c, s_xc)
 
         cuts = first_sends(
-            me, block_adapter, rank_per_adapter, block_rows, tokens, grad_out,
-            after(up, s_keep), outer,
+            me, block_adapter, rank_per_adapter, tokens, after(up, s_keep), grads, outer
         )
         xe = to_planes(cuts)
 
         low = shrink_parts(me, sparts, xe, outer)
-        held_t, held_f, *sends = main_parts(me, wparts, sparts, after(xe, low), outer)
+        products = main_parts(
+            me, wparts, sparts, after(xe, low), grads, evens, outer
+        )
+        sends, held_f = products[:outer], products[outer]
+        even_f, odd_f = products[outer + 1 : -1], products[-1]
+        odd_got = swap(odd_f, INNER)
         low = to_planes(low)
         extra, eg = shrunk_rows(
-            me, block_adapter, rank_per_adapter, after(low, sends), up, cuts[0]
+            me, block_adapter, rank_per_adapter, after(low, products), up, masked
         )
         eg_got = eg.reshape(devices, rank // devices, kv)
         eg_got = lax.all_to_all(eg_got, "fsdp", split_axis=0, concat_axis=0, tiled=True)
@@ -428,9 +490,13 @@
         packed = [p if j == 0 else swap(p, j) for j, p in enumerate(packed)]
         shrink_grad = down_grad(me, block_adapter, packed, adapters, rank)
         expand_grad = up_grad(after(block_adapter, shrink_grad), eg_got, adapters)
-        got = to_planes([held_t] + sends)[1:]
+        parts = []
+        for i, value in enumerate(even_f):
+            value = value + odd_got[i * BLOCK : (i + 1) * BLOCK].astype(F32)
+            parts.append(swap(value.astype(BF), 2 * (i + 1) * INNER))
+        held_t, *got = to_planes(sends)
         projected, token_input_gradient = join(
-            me, held_t, held_f, extra, after(got, expand_grad)
+            me, held_t, held_f, extra, after(got, expand_grad), parts
         )
         return (projected, token_input_gradient, shrink_grad, expand_grad)
 

time: 201 us -> 182 us (0.905)
  waiting for transfers between devices: 111 us -> 84.5 us
  starting transfers between devices: 40.2 us -> 47.6 us
    ppermute x19 -> x22, waiting for transfers between devices: 79.7 us -> 61 us  [swap(): return lax.ppermute(value, 'fsdp', [(i, i ^ mask) for i in range(devices)])]
    ppermute x19 -> x22, starting transfers between devices: 28 us -> 32.8 us  [swap(): return lax.ppermute(value, 'fsdp', [(i, i ^ mask) for i in range(devices)])]
    all_to_all x1, waiting for transfers between devices: 4.17 us -> 0.01 us  [on_device(): lax.all_to_all(up_send, 'fsdp', split_axis=0, concat_axis=0, tiled=True)]
    all_to_all x1, waiting for transfers between devices: 26.9 us -> 23.5 us  [on_device(): lax.all_to_all(eg_got, 'fsdp', split_axis=0, concat_axis=0, tiled=True)]
    all_to_all x1, starting transfers between devices: 5.72 us -> 8.21 us  [on_device(): lax.all_to_all(eg_got, 'fsdp', split_axis=0, concat_axis=0, tiled=True)]
    pallas_call x2 -> x3, Pallas kernels: 11.1 us -> 10.7 us  [the longest x1 9.79 us: main_parts(): pl.pallas_call(lambda *refs: main_kernel(evens, outer, sub, kv, *refs), o...]
  transfers between devices with their start and end apart: 21 -> 24, of which waited for: 7 -> 6; matrix products, arithmetic and copies ran while one was open for 1% -> 1% of each run, Pallas kernels for 17% -> 19%
where the time goes in v2:
time: 182 us; the launch traced here: 179 us
  waiting for transfers between devices  84.5 us (46%)
  starting transfers between devices  47.6 us (26%)
  Pallas kernels  38.7 us (21%)
  local copies, waits for them, and re-layouts  4.16 us (2%)
  other arithmetic  2.53 us (1%)
    ppermute x22, waiting for transfers between devices, swap(): return lax.ppermute(value, 'fsdp', [(i, i ^ mask) for i in range(devices)])  61 us
    ppermute x22, starting transfers between devices, swap(): return lax.ppermute(value, 'fsdp', [(i, i ^ mask) for i in range(devices)])  32.8 us
    all_to_all x1, waiting for transfers between devices, on_device(): lax.all_to_all(eg_got, 'fsdp', split_axis=0, concat_axis=0, tiled=True)  23.5 us
    pallas_call x1, Pallas kernels, down_grad(): pl.pallas_call(lambda *refs: down_kernel(per, blocks, rank, *refs), grid_...  15.5 us
    pallas_call x1, Pallas kernels, main_parts(): pl.pallas_call(lambda *refs: main_kernel(evens, outer, sub, kv, *refs), o...  9.79 us
    all_to_all x1, starting transfers between devices, on_device(): lax.all_to_all(eg_got, 'fsdp', split_axis=0, concat_axis=0, tiled=True)  8.21 us
    all_to_all x1, starting transfers between devices, on_device(): lax.all_to_all(up_send, 'fsdp', split_axis=0, concat_axis=0, tiled=True)  6.55 us
    pallas_call x1, Pallas kernels, pick(): pl.pallas_call(lambda *refs: pick_kernel(outer, *refs), out_shape=(picked...  3.74 us
  transfers between devices with their start and end apart: 24, of which 6 were waited for; matrix products, arithmetic and copies ran while one was open for 1% of the time, Pallas kernels for 19%

profile of v2, /device:TPU:11, one launch (start us, length us, event | category | flops | bytes accessed | tf_op | source)
XLA Modules:
  0.0 179.1 jit_solution(271889311887366481)
XLA Ops:
  1.4 0.9 copy-done.17
  3.0 1.3 gather_fusion
  4.3 6.6 %all-to-all-start = ((bf16[16,8,1024]{2,1,0:T(8,128)(2,1)}), bf16[16,8,1024]{2,1,0:T(8,128)(2,1)S(1)}, u32[]{:S(2)}, u32[]{:S(2)}) async-start(bf16[16,8,1024]{2,1,0:T(8,128)(2,1)} %gather_fusion), calls=%async_computation | async-start | bytes 524288 | tf_op jit(solution)/shard_map/all_to_all | solution.py:457
  10.9 2.1 %collective-permute-start = (bf16[128,1024]{1,0:T(8,128)(2,1)S(1)}, bf16[128,1024]{1,0:T(8,128)(2,1)S(1)}, u32[]{:S(2)}, u32[]{:S(2)}) collective-permute-start(bf16[128,1024]{1,0:T(8,128)(2,1)S(1)} %mask_rows.1.refs_5_.refs_14_.refs_8_), channel_id=1, source_target_pairs={{0,8},{1,9},{2,10},{3,11},{4,12},{5,13},{6,14},{7,15},{8,0},{9,1},... | collective-permute-start | bytes 786440 | tf_op jit(solution)/shard_map/ppermute | solution.py:432
  13.0 3.7 %pick_factors.1 = (bf16[8,512,128]{2,1,0:T(8,128)(2,1)}, bf16[8,512,128]{2,1,0:T(8,128)(2,1)}) custom-call(s32[1]{0:T(128)} %bitcast.refs_0_, s32[16]{0:T(128)} %refs_0_, bf16[64,512,128]{2,1,0:T(8,128)(2,1)} %refs_2_.3), custom_call_target="tpu_custom_call" | custom-call | flops 1 | bytes 1 | tf_op jit(solution)/shard_map/pick_factors/pallas_call | solution.py:52
  16.7 11.4 %collective-permute-done.refs_6_.refs_15_ = bf16[128,1024]{1,0:T(8,128)(2,1)S(1)} collective-permute-done((bf16[128,1024]{1,0:T(8,128)(2,1)S(1)}, bf16[128,1024]{1,0:T(8,128)(2,1)S(1)}, u32[]{:S(2)}, u32[]{:S(2)}) %collective-permute-start) | collective-permute-done | bytes 262176 | tf_op jit(solution)/shard_map/ppermute | solution.py:432
  28.4 1.3 collective-permute-start.5
  29.6 1.6 copy-done.9
  31.2 0.9 first_sends.1
  32.1 3.0 %collective-permute-start.8 = (bf16[128,4224]{1,0:T(8,128)(2,1)S(1)}, bf16[128,4224]{1,0:T(8,128)(2,1)S(1)}, u32[]{:S(2)}, u32[]{:S(2)}) collective-permute-start(bf16[128,4224]{1,0:T(8,128)(2,1)S(1)} %get-tuple-element.62), channel_id=1, source_target_pairs={{0,4},{1,5},{2,6},{3,7},{4,0},{5,1},{6,2},{7,3},{8,12},{9,13},{10,... | collective-permute-start | bytes 3244040 | tf_op jit(solution)/shard_map/ppermute | solution.py:432
  35.4 1.0 collective-permute-start.10
  36.3 16.1 %collective-permute-done.1.refs_3_ = bf16[512,1024]{1,0:T(8,128)(2,1)S(1)} collective-permute-done((bf16[512,1024]{1,0:T(8,128)(2,1)}, bf16[512,1024]{1,0:T(8,128)(2,1)S(1)}, u32[]{:S(2)}, u32[]{:S(2)}) %collective-permute-start.1) | collective-permute-done | bytes 1048608 | tf_op jit(solution)/shard_map/ppermute | solution.py:432
  52.4 2.7 %collective-permute-start.2 = (bf16[512,1024]{1,0:T(8,128)(2,1)S(1)}, bf16[512,1024]{1,0:T(8,128)(2,1)}, u32[]{:S(2)}, u32[]{:S(2)}) collective-permute-start(bf16[512,1024]{1,0:T(8,128)(2,1)S(1)} %copy-done.22), channel_id=1, source_target_pairs={{0,1},{1,0},{2,3},{3,2},{4,5},{5,4},{6,7},{7,6},{8,9},{9,8},{10,11... | collective-permute-start | bytes 3145736 | tf_op jit(solution)/shard_map/ppermute | solution.py:432
  55.1 19.8 %collective-permute-done.5.refs_2_.refs_7_ = bf16[8,512,128]{2,1,0:T(8,128)(2,1)S(1)} collective-permute-done((bf16[8,512,128]{2,1,0:T(8,128)(2,1)}, bf16[8,512,128]{2,1,0:T(8,128)(2,1)S(1)}, u32[]{:S(2)}, u32[]{:S(2)}) %collective-permute-start.5) | collective-permute-done | bytes 1048608 | tf_op jit(solution)/shard_map/ppermute | solution.py:432
  75.0 1.6 collective-permute-start.7
  76.8 9.0 %collective-permute-start.4 = (bf16[256,1024]{1,0:T(8,128)(2,1)S(1)}, bf16[256,1024]{1,0:T(8,128)(2,1)S(1)}, u32[]{:S(2)}, u32[]{:S(2)}) collective-permute-start(bf16[256,1024]{1,0:T(8,128)(2,1)S(1)} %get-tuple-element.100), channel_id=1, source_target_pairs={{0,1},{1,0},{2,3},{3,2},{4,5},{5,4},{6,7},{7,6},{8,9},{9,8},{10,11... | collective-permute-start | bytes 1572872 | tf_op jit(solution)/shard_map/ppermute | solution.py:432
  86.8 1.7 collective-permute-start.12
  88.4 1.0 collective-permute-start.13
  89.4 9.8 %plane_products.1 = (bf16[128,2048]{1,0:T(8,128)(2,1)S(1)}, bf16[128,3072]{1,0:T(8,128)(2,1)}, bf16[128,2048]{1,0:T(8,128)(2,1)}, bf16[128,2048]{1,0:T(8,128)(2,...) custom-call(s32[1]{0:T(128)} %bitcast.refs_0_, bf16[512,1024]{1,0:T(8,128)(2,1)} %refs_1_.6, ...), custom_call_target="tpu_custom_call" | custom-call | flops 1 | bytes 1 | tf_op jit(solution)/shard_map/plane_products/pallas_call | solution.py:211
  100.2 1.3 pack_columns.1
  101.5 1.2 collective-permute-start.17
  104.5 1.9 %collective-permute-start.19 = (bf16[512,640]{1,0:T(8,128)(2,1)}, bf16[512,640]{1,0:T(8,128)(2,1)}, u32[]{:S(2)}, u32[]{:S(2)}) collective-permute-start(bf16[512,640]{1,0:T(8,128)(2,1)} %get-tuple-element.93), channel_id=1, source_target_pairs={{0,3},{1,2},{2,1},{3,0},{4,7},{5,6},{6,5},{7,4},{8,11},{9,10},{10,... | collective-permute-start | bytes 1966088 | tf_op jit(solution)/shard_map/ppermute | solution.py:432
  106.4 4.3 %collective-permute-done.20 = bf16[128,1024]{1,0:T(8,128)(2,1)} collective-permute-done((bf16[128,1024]{1,0:T(8,128)(2,1)S(1)}, bf16[128,1024]{1,0:T(8,128)(2,1)}, u32[]{:S(2)}, u32[]{:S(2)}) %collective-permute-start.20) | collective-permute-done | bytes 262176 | tf_op jit(solution)/shard_map/ppermute | solution.py:432
  110.7 1.1 collective-permute-start.15
  112.6 8.2 %all-to-all-start.1 = ((bf16[16,8,1024]{2,1,0:T(8,128)(2,1)}), bf16[16,8,1024]{2,1,0:T(8,128)(2,1)S(1)}, u32[]{:S(2)}, u32[]{:S(2)}) async-start(bf16[16,8,1024]{2,1,0:T(8,128)(2,1)} %bitcast.5), calls=%async_computation.1 | async-start | bytes 524288 | tf_op jit(solution)/shard_map/all_to_all | solution.py:487
  120.8 1.9 %add_convert_fusion = bf16[128,1024]{1,0:T(8,128)(2,1)} fusion(f32[128,1024]{1,0:T(8,128)} %copy-done.10, bf16[128,1024]{1,0:T(8,128)(2,1)} %collective-permute-done.20), kind=kLoop, calls=%fused_computation.1 | loop fusion | flops 393216 | bytes 1048576 | tf_op jit(solution)/shard_map/convert_element_type | solution.py:496
  122.7 2.1 %collective-permute-start.21 = (bf16[128,1024]{1,0:T(8,128)(2,1)}, bf16[128,1024]{1,0:T(8,128)(2,1)}, u32[]{:S(2)}, u32[]{:S(2)}) collective-permute-start(bf16[128,1024]{1,0:T(8,128)(2,1)} %add_convert_fusion), channel_id=1, source_target_pairs={{0,8},{1,9},{2,10},{3,11},{4,12},{5,13},{6,14},{7,15},{8,0},{9,1},... | collective-permute-start | bytes 786440 | tf_op jit(solution)/shard_map/ppermute | solution.py:432
  124.9 9.3 %collective-permute-done.19.refs_5_ = bf16[512,640]{1,0:T(8,128)(2,1)} collective-permute-done((bf16[512,640]{1,0:T(8,128)(2,1)}, bf16[512,640]{1,0:T(8,128)(2,1)}, u32[]{:S(2)}, u32[]{:S(2)}) %collective-permute-start.19) | collective-permute-done | bytes 655392 | tf_op jit(solution)/shard_map/ppermute | solution.py:432
  134.2 15.5 %down_gradient.1 = f32[64,512,128]{2,1,0:T(8,128)} custom-call(s32[1]{0:T(128)} %bitcast.refs_0_, s32[16]{0:T(128)S(1)} %copy-done.19, bf16[512,640]{1,0:T(8,128)(2,1)S(1)} %get-tuple-element.90.refs_2_, bf16[512,640]{1,0:T(8,128)(2,1)S(1)} %collective-permute-done.17.refs_3_, bf16[512,640]{1,0:T(8,128)(2,1)} %collective-permute-done.18.refs_4_, ...), custom_call_target="tpu_custom_call" | custom-call | flops 1 | bytes 1 | tf_op jit(solution)/shard_map/down_gradient/pallas_call | solution.py:352
  149.7 23.5 %all-to-all-done.1.refs_1_ = bf16[16,8,1024]{2,1,0:T(8,128)(2,1)S(1)} async-done(((bf16[16,8,1024]{2,1,0:T(8,128)(2,1)}), bf16[16,8,1024]{2,1,0:T(8,128)(2,1)S(1)}, u32[]{:S(2)}, u32[]{:S(2)}) %all-to-all-start.1) | async-done | bytes 262176 | tf_op jit(solution)/shard_map/all_to_all | solution.py:487
  173.2 3.0 %up_gradient.1 = f32[64,8,1024]{2,1,0:T(8,128)} custom-call(s32[16]{0:T(128)S(1)} %copy-done.19, bf16[16,8,1024]{2,1,0:T(8,128)(2,1)S(1)} %all-to-all-done.1.refs_1_), custom_call_target="tpu_custom_call" | custom-call | flops 1 | bytes 1 | tf_op jit(solution)/shard_map/up_gradient/pallas_call | solution.py:386
  176.2 2.9 %join_columns.1 = (bf16[128,1024]{1,0:T(8,128)(2,1)}, bf16[128,8192]{1,0:T(8,128)(2,1)}) custom-call(s32[1]{0:T(128)} %bitcast.refs_0_, bf16[128,2048]{1,0:T(8,128)(2,1)S(1)} %copy-done.12, f32[128,1024]{1,0:T(8,128)S(1)} %copy-done.14, f32[128,1024]{1,0:T(8,128)S(1)} %copy-done.16, bf16[128,3072]{1,0:T(8,128)(2,1)S(1)} %collective-permute-done.14.refs_4_, ...), custom_call_target="tpu_custom_call" | custom-call | flops 1 | bytes 1 | tf_op jit(solution)/shard_map/join_columns/pallas_call | solution.py:414
  (78 shorter events, 5.9 us)
Async XLA Ops:
  4.3 23.8 %all-to-all-start = ((bf16[16,8,1024]{2,1,0:T(8,128)(2,1)}), bf16[16,8,1024]{2,1,0:T(8,128)(2,1)S(1)}, u32[]{:S(2)}, u32[]{:S(2)}) async-start(bf16[16,8,1024]{2,1,0:T(8,128)(2,1)} %gather_fusion), calls=%async_computation | async-start | bytes 524288 | tf_op jit(solution)/shard_map/all_to_all | solution.py:457
  10.9 17.3 %collective-permute-start = (bf16[128,1024]{1,0:T(8,128)(2,1)S(1)}, bf16[128,1024]{1,0:T(8,128)(2,1)S(1)}, u32[]{:S(2)}, u32[]{:S(2)}) collective-permute-start(bf16[128,1024]{1,0:T(8,128)(2,1)S(1)} %mask_rows.1.refs_5_.refs_14_.refs_8_), channel_id=1, source_target_pairs={{0,8},{1,9},{2,10},{3,11},{4,12},{5,13},{6,14},{7,15},{8,0},{9,1},... | collective-permute-start | bytes 786440 | tf_op jit(solution)/shard_map/ppermute | solution.py:432
  13.0 16.7 %copy-start.19 = (s32[16]{0:T(128)S(1)}, s32[16]{0:T(128)}, u32[]{:S(2)}) copy-start(s32[16]{0:T(128)} %refs_0_) | copy-start | bytes 196
  13.0 16.7 %copy-start.20 = (s32[64]{0:T(128)S(1)}, s32[64]{0:T(128)}, u32[]{:S(2)}) copy-start(s32[64]{0:T(128)} %refs_2_.5) | copy-start | bytes 772
  16.7 58.2 %copy-start.3 = (bf16[8,512,128]{2,1,0:T(8,128)(2,1)S(1)}, bf16[8,512,128]{2,1,0:T(8,128)(2,1)}, u32[]{:S(2)}) copy-start(bf16[8,512,128]{2,1,0:T(8,128)(2,1)} %get-tuple-element.59.refs_1_.refs_6_) | copy-start | bytes 3145732
  28.2 24.2 %collective-permute-start.1 = (bf16[512,1024]{1,0:T(8,128)(2,1)}, bf16[512,1024]{1,0:T(8,128)(2,1)S(1)}, u32[]{:S(2)}, u32[]{:S(2)}) collective-permute-start(bf16[512,1024]{1,0:T(8,128)(2,1)} %refs_1_.6), channel_id=1, source_target_pairs={{0,2},{1,3},{2,0},{3,1},{4,6},{5,7},{6,4},{7,5},{8,10},{9,11},{10,... | collective-permute-start | bytes 3145736 | tf_op jit(solution)/shard_map/ppermute | solution.py:432
  28.4 46.5 %collective-permute-start.5 = (bf16[8,512,128]{2,1,0:T(8,128)(2,1)}, bf16[8,512,128]{2,1,0:T(8,128)(2,1)S(1)}, u32[]{:S(2)}, u32[]{:S(2)}) collective-permute-start(bf16[8,512,128]{2,1,0:T(8,128)(2,1)} %get-tuple-element.58), channel_id=1, source_target_pairs={{0,2},{1,3},{2,0},{3,1},{4,6},{5,7},{6,4},{7,5},{8,10},{9,11},{10,... | collective-permute-start | bytes 3145736 | tf_op jit(solution)/shard_map/ppermute | solution.py:432
  31.2 21.2 %copy-start.22 = (bf16[512,1024]{1,0:T(8,128)(2,1)S(1)}, bf16[512,1024]{1,0:T(8,128)(2,1)}, u32[]{:S(2)}) copy-start(bf16[512,1024]{1,0:T(8,128)(2,1)} %refs_1_.6) | copy-start | bytes 3145732
  32.1 53.7 %collective-permute-start.8 = (bf16[128,4224]{1,0:T(8,128)(2,1)S(1)}, bf16[128,4224]{1,0:T(8,128)(2,1)S(1)}, u32[]{:S(2)}, u32[]{:S(2)}) collective-permute-start(bf16[128,4224]{1,0:T(8,128)(2,1)S(1)} %get-tuple-element.62), channel_id=1, source_target_pairs={{0,4},{1,5},{2,6},{3,7},{4,0},{5,1},{6,2},{7,3},{8,12},{9,13},{10,... | collective-permute-start | bytes 3244040 | tf_op jit(solution)/shard_map/ppermute | solution.py:432
  35.1 41.5 %collective-permute-start.9 = (bf16[128,2176]{1,0:T(8,128)(2,1)S(1)}, bf16[128,2176]{1,0:T(8,128)(2,1)S(1)}, u32[]{:S(2)}, u32[]{:S(2)}) collective-permute-start(bf16[128,2176]{1,0:T(8,128)(2,1)S(1)} %get-tuple-element.63), channel_id=1, source_target_pairs={{0,8},{1,9},{2,10},{3,11},{4,12},{5,13},{6,14},{7,15},{8,0},{9,1},... | collective-permute-start | bytes 1671176 | tf_op jit(solution)/shard_map/ppermute | solution.py:432
  35.4 41.4 %collective-permute-start.10 = (bf16[128,2176]{1,0:T(8,128)(2,1)S(1)}, bf16[128,2176]{1,0:T(8,128)(2,1)S(1)}, u32[]{:S(2)}, u32[]{:S(2)}) collective-permute-start(bf16[128,2176]{1,0:T(8,128)(2,1)S(1)} %get-tuple-element.64), channel_id=1, source_target_pairs={{0,12},{1,13},{2,14},{3,15},{4,8},{5,9},{6,10},{7,11},{8,4},{9,5},... | collective-permute-start | bytes 1671176 | tf_op jit(solution)/shard_map/ppermute | solution.py:432
  52.4 24.3 %copy-start.21 = (bf16[512,1024]{1,0:T(8,128)(2,1)}, bf16[512,1024]{1,0:T(8,128)(2,1)S(1)}, u32[]{:S(2)}) copy-start(bf16[512,1024]{1,0:T(8,128)(2,1)S(1)} %collective-permute-done.1.refs_3_) | copy-start | bytes 3145732
  52.4 37.0 %collective-permute-start.2 = (bf16[512,1024]{1,0:T(8,128)(2,1)S(1)}, bf16[512,1024]{1,0:T(8,128)(2,1)}, u32[]{:S(2)}, u32[]{:S(2)}) collective-permute-start(bf16[512,1024]{1,0:T(8,128)(2,1)S(1)} %copy-done.22), channel_id=1, source_target_pairs={{0,1},{1,0},{2,3},{3,2},{4,5},{5,4},{6,7},{7,6},{8,9},{9,8},{10,11... | collective-permute-start | bytes 3145736 | tf_op jit(solution)/shard_map/ppermute | solution.py:432
  75.0 10.9 %collective-permute-start.7 = (bf16[4,512,128]{2,1,0:T(8,128)(2,1)S(1)}, bf16[4,512,128]{2,1,0:T(8,128)(2,1)S(1)}, u32[]{:S(2)}, u32[]{:S(2)}) collective-permute-start(bf16[4,512,128]{2,1,0:T(8,128)(2,1)S(1)} %slice.20), channel_id=1, source_target_pairs={{0,1},{1,0},{2,3},{3,2},{4,5},{5,4},{6,7},{7,6},{8,9},{9,8},{10,11... | collective-permute-start | bytes 1572872 | tf_op jit(solution)/shard_map/ppermute | solution.py:432
  76.6 9.3 %collective-permute-start.6 = (bf16[4,512,128]{2,1,0:T(8,128)(2,1)S(1)}, bf16[4,512,128]{2,1,0:T(8,128)(2,1)S(1)}, u32[]{:S(2)}, u32[]{:S(2)}) collective-permute-start(bf16[4,512,128]{2,1,0:T(8,128)(2,1)S(1)} %slice.14), channel_id=1, source_target_pairs={{0,1},{1,0},{2,3},{3,2},{4,5},{5,4},{6,7},{7,6},{8,9},{9,8},{10,11... | collective-permute-start | bytes 1572872 | tf_op jit(solution)/shard_map/ppermute | solution.py:432
  76.8 11.7 %collective-permute-start.4 = (bf16[256,1024]{1,0:T(8,128)(2,1)S(1)}, bf16[256,1024]{1,0:T(8,128)(2,1)S(1)}, u32[]{:S(2)}, u32[]{:S(2)}) collective-permute-start(bf16[256,1024]{1,0:T(8,128)(2,1)S(1)} %get-tuple-element.100), channel_id=1, source_target_pairs={{0,1},{1,0},{2,3},{3,2},{4,5},{5,4},{6,7},{7,6},{8,9},{9,8},{10,11... | collective-permute-start | bytes 1572872 | tf_op jit(solution)/shard_map/ppermute | solution.py:432
  85.8 3.6 %collective-permute-start.3 = (bf16[256,1024]{1,0:T(8,128)(2,1)S(1)}, bf16[256,1024]{1,0:T(8,128)(2,1)S(1)}, u32[]{:S(2)}, u32[]{:S(2)}) collective-permute-start(bf16[256,1024]{1,0:T(8,128)(2,1)S(1)} %get-tuple-element.101), channel_id=1, source_target_pairs={{0,1},{1,0},{2,3},{3,2},{4,5},{5,4},{6,7},{7,6},{8,9},{9,8},{10,11... | collective-permute-start | bytes 1572872 | tf_op jit(solution)/shard_map/ppermute | solution.py:432
  86.8 12.5 %collective-permute-start.11 = (f32[128,128]{1,0:T(8,128)S(1)}, f32[128,128]{1,0:T(8,128)S(1)}, u32[]{:S(2)}, u32[]{:S(2)}) collective-permute-start(f32[128,128]{1,0:T(8,128)S(1)} %get-tuple-element.66), channel_id=1, source_target_pairs={{0,4},{1,5},{2,6},{3,7},{4,0},{5,1},{6,2},{7,3},{8,12},{9,13},{10,... | collective-permute-start | bytes 196616 | tf_op jit(solution)/shard_map/ppermute | solution.py:432
  86.8 12.5 %collective-permute-start.12 = (f32[128,128]{1,0:T(8,128)S(1)}, f32[128,128]{1,0:T(8,128)S(1)}, u32[]{:S(2)}, u32[]{:S(2)}) collective-permute-start(f32[128,128]{1,0:T(8,128)S(1)} %get-tuple-element.67), channel_id=1, source_target_pairs={{0,8},{1,9},{2,10},{3,11},{4,12},{5,13},{6,14},{7,15},{8,0},{9,1},... | collective-permute-start | bytes 196616 | tf_op jit(solution)/shard_map/ppermute | solution.py:432
  88.4 10.8 %collective-permute-start.13 = (f32[128,128]{1,0:T(8,128)S(1)}, f32[128,128]{1,0:T(8,128)S(1)}, u32[]{:S(2)}, u32[]{:S(2)}) collective-permute-start(f32[128,128]{1,0:T(8,128)S(1)} %get-tuple-element.68), channel_id=1, source_target_pairs={{0,12},{1,13},{2,14},{3,15},{4,8},{5,9},{6,10},{7,11},{8,4},{9,5},... | collective-permute-start | bytes 196616 | tf_op jit(solution)/shard_map/ppermute | solution.py:432
  99.2 13.4 %copy-start.11 = (bf16[128,2048]{1,0:T(8,128)(2,1)}, bf16[128,2048]{1,0:T(8,128)(2,1)S(1)}, u32[]{:S(2)}) copy-start(bf16[128,2048]{1,0:T(8,128)(2,1)S(1)} %get-tuple-element.73.refs_1_) | copy-start | bytes 1572868
  101.5 10.3 %collective-permute-start.17 = (bf16[512,640]{1,0:T(8,128)(2,1)S(1)}, bf16[512,640]{1,0:T(8,128)(2,1)S(1)}, u32[]{:S(2)}, u32[]{:S(2)}) collective-permute-start(bf16[512,640]{1,0:T(8,128)(2,1)S(1)} %get-tuple-element.91), channel_id=1, source_target_pairs={{0,1},{1,0},{2,3},{3,2},{4,5},{5,4},{6,7},{7,6},{8,9},{9,8},{10,11... | collective-permute-start | bytes 1966088 | tf_op jit(solution)/shard_map/ppermute | solution.py:432
  102.7 20.0 %collective-permute-start.18 = (bf16[512,640]{1,0:T(8,128)(2,1)}, bf16[512,640]{1,0:T(8,128)(2,1)}, u32[]{:S(2)}, u32[]{:S(2)}) collective-permute-start(bf16[512,640]{1,0:T(8,128)(2,1)} %get-tuple-element.92), channel_id=1, source_target_pairs={{0,2},{1,3},{2,0},{3,1},{4,6},{5,7},{6,4},{7,5},{8,10},{9,11},{10,... | collective-permute-start | bytes 1966088 | tf_op jit(solution)/shard_map/ppermute | solution.py:432
  103.0 7.7 %collective-permute-start.20 = (bf16[128,1024]{1,0:T(8,128)(2,1)S(1)}, bf16[128,1024]{1,0:T(8,128)(2,1)}, u32[]{:S(2)}, u32[]{:S(2)}) collective-permute-start(bf16[128,1024]{1,0:T(8,128)(2,1)S(1)} %get-tuple-element.79), channel_id=1, source_target_pairs={{0,4},{1,5},{2,6},{3,7},{4,0},{5,1},{6,2},{7,3},{8,12},{9,13},{10,... | collective-permute-start | bytes 786440 | tf_op jit(solution)/shard_map/ppermute | solution.py:432
  103.7 72.5 %collective-permute-start.14 = (bf16[128,3072]{1,0:T(8,128)(2,1)}, bf16[128,3072]{1,0:T(8,128)(2,1)S(1)}, u32[]{:S(2)}, u32[]{:S(2)}) collective-permute-start(bf16[128,3072]{1,0:T(8,128)(2,1)} %get-tuple-element.75), channel_id=1, source_target_pairs={{0,4},{1,5},{2,6},{3,7},{4,0},{5,1},{6,2},{7,3},{8,12},{9,13},{10,... | collective-permute-start | bytes 2359304 | tf_op jit(solution)/shard_map/ppermute | solution.py:432
  104.5 29.7 %collective-permute-start.19 = (bf16[512,640]{1,0:T(8,128)(2,1)}, bf16[512,640]{1,0:T(8,128)(2,1)}, u32[]{:S(2)}, u32[]{:S(2)}) collective-permute-start(bf16[512,640]{1,0:T(8,128)(2,1)} %get-tuple-element.93), channel_id=1, source_target_pairs={{0,3},{1,2},{2,1},{3,0},{4,7},{5,6},{6,5},{7,4},{8,11},{9,10},{10,... | collective-permute-start | bytes 1966088 | tf_op jit(solution)/shard_map/ppermute | solution.py:432
  110.7 65.5 %collective-permute-start.15 = (bf16[128,2048]{1,0:T(8,128)(2,1)}, bf16[128,2048]{1,0:T(8,128)(2,1)}, u32[]{:S(2)}, u32[]{:S(2)}) collective-permute-start(bf16[128,2048]{1,0:T(8,128)(2,1)} %get-tuple-element.76), channel_id=1, source_target_pairs={{0,8},{1,9},{2,10},{3,11},{4,12},{5,13},{6,14},{7,15},{8,0},{9,1},... | collective-permute-start | bytes 1572872 | tf_op jit(solution)/shard_map/ppermute | solution.py:432
  111.8 64.4 %collective-permute-start.16 = (bf16[128,2048]{1,0:T(8,128)(2,1)}, bf16[128,2048]{1,0:T(8,128)(2,1)}, u32[]{:S(2)}, u32[]{:S(2)}) collective-permute-start(bf16[128,2048]{1,0:T(8,128)(2,1)} %get-tuple-element.77), channel_id=1, source_target_pairs={{0,12},{1,13},{2,14},{3,15},{4,8},{5,9},{6,10},{7,11},{8,4},{9,5},... | collective-permute-start | bytes 1572872 | tf_op jit(solution)/shard_map/ppermute | solution.py:432
  112.6 60.5 %all-to-all-start.1 = ((bf16[16,8,1024]{2,1,0:T(8,128)(2,1)}), bf16[16,8,1024]{2,1,0:T(8,128)(2,1)S(1)}, u32[]{:S(2)}, u32[]{:S(2)}) async-start(bf16[16,8,1024]{2,1,0:T(8,128)(2,1)} %bitcast.5), calls=%async_computation.1 | async-start | bytes 524288 | tf_op jit(solution)/shard_map/all_to_all | solution.py:487
  122.7 53.5 %collective-permute-start.21 = (bf16[128,1024]{1,0:T(8,128)(2,1)}, bf16[128,1024]{1,0:T(8,128)(2,1)}, u32[]{:S(2)}, u32[]{:S(2)}) collective-permute-start(bf16[128,1024]{1,0:T(8,128)(2,1)} %add_convert_fusion), channel_id=1, source_target_pairs={{0,8},{1,9},{2,10},{3,11},{4,12},{5,13},{6,14},{7,15},{8,0},{9,1},... | collective-permute-start | bytes 786440 | tf_op jit(solution)/shard_map/ppermute | solution.py:432
  149.7 26.5 %copy-start.12 = (bf16[128,2048]{1,0:T(8,128)(2,1)S(1)}, bf16[128,2048]{1,0:T(8,128)(2,1)}, u32[]{:S(2)}) copy-start(bf16[128,2048]{1,0:T(8,128)(2,1)} %copy-done.11) | copy-start | bytes 1572868
  149.7 26.5 %copy-start.14 = (f32[128,1024]{1,0:T(8,128)S(1)}, f32[128,1024]{1,0:T(8,128)}, u32[]{:S(2)}) copy-start(f32[128,1024]{1,0:T(8,128)} %copy-done.13) | copy-start | bytes 1572868
  (15 other events, 123.1 us)

commit v3 on v2

--- a/solution.py
+++ b/solution.py
@@ -487,7 +487,9 @@
         eg_got = lax.all_to_all(eg_got, "fsdp", split_axis=0, concat_axis=0, tiled=True)
 
         packed = pack(me, after(xe, eg), sub, rank, outer)
-        packed = [p if j == 0 else swap(p, j) for j, p in enumerate(packed)]
+        core = swap(packed[1], 1)
+        far = after(packed[2:], core)
+        packed = [packed[0], core] + [swap(p, 2 + j) for j, p in enumerate(far)]
         shrink_grad = down_grad(me, block_adapter, packed, adapters, rank)
         expand_grad = up_grad(after(block_adapter, shrink_grad), eg_got, adapters)
         parts = []

time: 182 us -> 182 us (level)
  waiting for transfers between devices: 84.5 us -> 72.2 us
  starting transfers between devices: 47.6 us -> 59.5 us
    all_to_all x1, starting transfers between devices: 8.21 us -> 20.2 us  [on_device(): lax.all_to_all(eg_got, 'fsdp', split_axis=0, concat_axis=0, tiled=True)]
    ppermute x22, waiting for transfers between devices: 61 us -> 51.5 us  [swap(): return lax.ppermute(value, 'fsdp', [(i, i ^ mask) for i in range(devices)])]
    all_to_all x1, waiting for transfers between devices: 23.5 us -> 20.6 us  [on_device(): lax.all_to_all(eg_got, 'fsdp', split_axis=0, concat_axis=0, tiled=True)]
where the time goes in v3:
time: 182 us; the launch traced here: 179 us
  waiting for transfers between devices  72.2 us (40%)
  starting transfers between devices  59.5 us (33%)
  Pallas kernels  38.8 us (21%)
  local copies, waits for them, and re-layouts  4.16 us (2%)
  other arithmetic  2.53 us (1%)
    ppermute x22, waiting for transfers between devices, swap(): return lax.ppermute(value, 'fsdp', [(i, i ^ mask) for i in range(devices)])  51.5 us
    ppermute x22, starting transfers between devices, swap(): return lax.ppermute(value, 'fsdp', [(i, i ^ mask) for i in range(devices)])  32.7 us
    all_to_all x1, waiting for transfers between devices, on_device(): lax.all_to_all(eg_got, 'fsdp', split_axis=0, concat_axis=0, tiled=True)  20.6 us
    all_to_all x1, starting transfers between devices, on_device(): lax.all_to_all(eg_got, 'fsdp', split_axis=0, concat_axis=0, tiled=True)  20.2 us
    pallas_call x1, Pallas kernels, down_grad(): pl.pallas_call(lambda *refs: down_kernel(per, blocks, rank, *refs), grid_...  15.5 us
    pallas_call x1, Pallas kernels, main_parts(): pl.pallas_call(lambda *refs: main_kernel(evens, outer, sub, kv, *refs), o...  9.79 us
    all_to_all x1, starting transfers between devices, on_device(): lax.all_to_all(up_send, 'fsdp', split_axis=0, concat_axis=0, tiled=True)  6.55 us
    pallas_call x1, Pallas kernels, pick(): pl.pallas_call(lambda *refs: pick_kernel(outer, *refs), out_shape=(picked...  3.74 us
  transfers between devices with their start and end apart: 24, of which 6 were waited for; matrix products, arithmetic and copies ran while one was open for 1% of the time, Pallas kernels for 19%

profile of v3, /device:TPU:11, one launch (start us, length us, event | category | flops | bytes accessed | tf_op | source)
XLA Modules:
  0.0 178.7 jit_solution(414561280978864591)
XLA Ops:
  1.4 0.9 copy-done.17
  3.0 1.3 gather_fusion
  4.3 6.6 %all-to-all-start = ((bf16[16,8,1024]{2,1,0:T(8,128)(2,1)}), bf16[16,8,1024]{2,1,0:T(8,128)(2,1)S(1)}, u32[]{:S(2)}, u32[]{:S(2)}) async-start(bf16[16,8,1024]{2,1,0:T(8,128)(2,1)} %gather_fusion), calls=%async_computation | async-start | bytes 524288 | tf_op jit(solution)/shard_map/all_to_all | solution.py:457
  10.9 2.1 %collective-permute-start = (bf16[128,1024]{1,0:T(8,128)(2,1)S(1)}, bf16[128,1024]{1,0:T(8,128)(2,1)S(1)}, u32[]{:S(2)}, u32[]{:S(2)}) collective-permute-start(bf16[128,1024]{1,0:T(8,128)(2,1)S(1)} %mask_rows.1.refs_5_.refs_14_.refs_8_), channel_id=1, source_target_pairs={{0,8},{1,9},{2,10},{3,11},{4,12},{5,13},{6,14},{7,15},{8,0},{9,1},... | collective-permute-start | bytes 786440 | tf_op jit(solution)/shard_map/ppermute | solution.py:432
  13.0 3.7 %pick_factors.1 = (bf16[8,512,128]{2,1,0:T(8,128)(2,1)}, bf16[8,512,128]{2,1,0:T(8,128)(2,1)}) custom-call(s32[1]{0:T(128)} %bitcast.refs_0_, s32[16]{0:T(128)} %refs_0_, bf16[64,512,128]{2,1,0:T(8,128)(2,1)} %refs_2_.3), custom_call_target="tpu_custom_call" | custom-call | flops 1 | bytes 1 | tf_op jit(solution)/shard_map/pick_factors/pallas_call | solution.py:52
  16.7 11.4 %collective-permute-done.refs_6_.refs_15_ = bf16[128,1024]{1,0:T(8,128)(2,1)S(1)} collective-permute-done((bf16[128,1024]{1,0:T(8,128)(2,1)S(1)}, bf16[128,1024]{1,0:T(8,128)(2,1)S(1)}, u32[]{:S(2)}, u32[]{:S(2)}) %collective-permute-start) | collective-permute-done | bytes 262176 | tf_op jit(solution)/shard_map/ppermute | solution.py:432
  28.4 1.3 collective-permute-start.5
  29.6 1.6 copy-done.9
  31.2 0.9 first_sends.1
  32.1 3.0 %collective-permute-start.8 = (bf16[128,4224]{1,0:T(8,128)(2,1)S(1)}, bf16[128,4224]{1,0:T(8,128)(2,1)S(1)}, u32[]{:S(2)}, u32[]{:S(2)}) collective-permute-start(bf16[128,4224]{1,0:T(8,128)(2,1)S(1)} %get-tuple-element.64), channel_id=1, source_target_pairs={{0,4},{1,5},{2,6},{3,7},{4,0},{5,1},{6,2},{7,3},{8,12},{9,13},{10,... | collective-permute-start | bytes 3244040 | tf_op jit(solution)/shard_map/ppermute | solution.py:432
  35.4 1.0 collective-permute-start.10
  36.3 16.1 %collective-permute-done.1.refs_3_ = bf16[512,1024]{1,0:T(8,128)(2,1)S(1)} collective-permute-done((bf16[512,1024]{1,0:T(8,128)(2,1)}, bf16[512,1024]{1,0:T(8,128)(2,1)S(1)}, u32[]{:S(2)}, u32[]{:S(2)}) %collective-permute-start.1) | collective-permute-done | bytes 1048608 | tf_op jit(solution)/shard_map/ppermute | solution.py:432
  52.4 2.7 %collective-permute-start.2 = (bf16[512,1024]{1,0:T(8,128)(2,1)S(1)}, bf16[512,1024]{1,0:T(8,128)(2,1)}, u32[]{:S(2)}, u32[]{:S(2)}) collective-permute-start(bf16[512,1024]{1,0:T(8,128)(2,1)S(1)} %copy-done.22), channel_id=1, source_target_pairs={{0,1},{1,0},{2,3},{3,2},{4,5},{5,4},{6,7},{7,6},{8,9},{9,8},{10,11... | collective-permute-start | bytes 3145736 | tf_op jit(solution)/shard_map/ppermute | solution.py:432
  55.1 19.8 %collective-permute-done.5.refs_2_.refs_7_ = bf16[8,512,128]{2,1,0:T(8,128)(2,1)S(1)} collective-permute-done((bf16[8,512,128]{2,1,0:T(8,128)(2,1)}, bf16[8,512,128]{2,1,0:T(8,128)(2,1)S(1)}, u32[]{:S(2)}, u32[]{:S(2)}) %collective-permute-start.5) | collective-permute-done | bytes 1048608 | tf_op jit(solution)/shard_map/ppermute | solution.py:432
  75.0 1.6 collective-permute-start.7
  76.8 9.0 %collective-permute-start.4 = (bf16[256,1024]{1,0:T(8,128)(2,1)S(1)}, bf16[256,1024]{1,0:T(8,128)(2,1)S(1)}, u32[]{:S(2)}, u32[]{:S(2)}) collective-permute-start(bf16[256,1024]{1,0:T(8,128)(2,1)S(1)} %get-tuple-element.104), channel_id=1, source_target_pairs={{0,1},{1,0},{2,3},{3,2},{4,5},{5,4},{6,7},{7,6},{8,9},{9,8},{10,11... | collective-permute-start | bytes 1572872 | tf_op jit(solution)/shard_map/ppermute | solution.py:432
  86.8 1.7 collective-permute-start.12
  88.4 1.0 collective-permute-start.13
  89.4 9.8 %plane_products.1 = (bf16[128,2048]{1,0:T(8,128)(2,1)S(1)}, bf16[128,3072]{1,0:T(8,128)(2,1)}, bf16[128,2048]{1,0:T(8,128)(2,1)}, bf16[128,2048]{1,0:T(8,128)(2,...) custom-call(s32[1]{0:T(128)} %bitcast.refs_0_, bf16[512,1024]{1,0:T(8,128)(2,1)} %refs_1_.6, ...), custom_call_target="tpu_custom_call" | custom-call | flops 1 | bytes 1 | tf_op jit(solution)/shard_map/plane_products/pallas_call | solution.py:211
  100.2 1.3 pack_columns.1
  101.5 1.2 collective-permute-start.17
  102.7 1.7 collective-permute-done.17.refs_3_
  106.2 2.3 %collective-permute-start.19 = (bf16[512,640]{1,0:T(8,128)(2,1)}, bf16[512,640]{1,0:T(8,128)(2,1)}, u32[]{:S(2)}, u32[]{:S(2)}) collective-permute-start(bf16[512,640]{1,0:T(8,128)(2,1)} %get-tuple-element.97), channel_id=1, source_target_pairs={{0,3},{1,2},{2,1},{3,0},{4,7},{5,6},{6,5},{7,4},{8,11},{9,10},{10,... | collective-permute-start | bytes 1966088 | tf_op jit(solution)/shard_map/ppermute | solution.py:432
  108.5 1.1 collective-permute-start.15
  109.6 2.5 %collective-permute-done.20 = bf16[128,1024]{1,0:T(8,128)(2,1)} collective-permute-done((bf16[128,1024]{1,0:T(8,128)(2,1)S(1)}, bf16[128,1024]{1,0:T(8,128)(2,1)}, u32[]{:S(2)}, u32[]{:S(2)}) %collective-permute-start.20) | collective-permute-done | bytes 262176 | tf_op jit(solution)/shard_map/ppermute | solution.py:432
  112.4 20.2 %all-to-all-start.1 = ((bf16[16,8,1024]{2,1,0:T(8,128)(2,1)}), bf16[16,8,1024]{2,1,0:T(8,128)(2,1)S(1)}, u32[]{:S(2)}, u32[]{:S(2)}) async-start(bf16[16,8,1024]{2,1,0:T(8,128)(2,1)} %bitcast.5), calls=%async_computation.1 | async-start | bytes 524288 | tf_op jit(solution)/shard_map/all_to_all | solution.py:487
  132.6 1.9 %add_convert_fusion = bf16[128,1024]{1,0:T(8,128)(2,1)} fusion(f32[128,1024]{1,0:T(8,128)} %copy-done.10, bf16[128,1024]{1,0:T(8,128)(2,1)} %collective-permute-done.20), kind=kLoop, calls=%fused_computation.1 | loop fusion | flops 393216 | bytes 1048576 | tf_op jit(solution)/shard_map/convert_element_type | solution.py:498
  134.5 2.1 %collective-permute-start.21 = (bf16[128,1024]{1,0:T(8,128)(2,1)}, bf16[128,1024]{1,0:T(8,128)(2,1)}, u32[]{:S(2)}, u32[]{:S(2)}) collective-permute-start(bf16[128,1024]{1,0:T(8,128)(2,1)} %add_convert_fusion), channel_id=1, source_target_pairs={{0,8},{1,9},{2,10},{3,11},{4,12},{5,13},{6,14},{7,15},{8,0},{9,1},... | collective-permute-start | bytes 786440 | tf_op jit(solution)/shard_map/ppermute | solution.py:432
  136.6 15.5 %down_gradient.1 = f32[64,512,128]{2,1,0:T(8,128)} custom-call(s32[1]{0:T(128)} %bitcast.refs_0_, s32[16]{0:T(128)S(1)} %copy-done.19, bf16[512,640]{1,0:T(8,128)(2,1)S(1)} %get-tuple-element.92.refs_2_, bf16[512,640]{1,0:T(8,128)(2,1)S(1)} %collective-permute-done.17.refs_3_, bf16[512,640]{1,0:T(8,128)(2,1)} %collective-permute-done.18.refs_4_, ...), custom_call_target="tpu_custom_call" | custom-call | flops 1 | bytes 1 | tf_op jit(solution)/shard_map/down_gradient/pallas_call | solution.py:352
  152.2 20.6 %all-to-all-done.1.refs_1_ = bf16[16,8,1024]{2,1,0:T(8,128)(2,1)S(1)} async-done(((bf16[16,8,1024]{2,1,0:T(8,128)(2,1)}), bf16[16,8,1024]{2,1,0:T(8,128)(2,1)S(1)}, u32[]{:S(2)}, u32[]{:S(2)}) %all-to-all-start.1) | async-done | bytes 262176 | tf_op jit(solution)/shard_map/all_to_all | solution.py:487
  172.8 3.0 %up_gradient.1 = f32[64,8,1024]{2,1,0:T(8,128)} custom-call(s32[16]{0:T(128)S(1)} %copy-done.19, bf16[16,8,1024]{2,1,0:T(8,128)(2,1)S(1)} %all-to-all-done.1.refs_1_), custom_call_target="tpu_custom_call" | custom-call | flops 1 | bytes 1 | tf_op jit(solution)/shard_map/up_gradient/pallas_call | solution.py:386
  175.9 2.9 %join_columns.1 = (bf16[128,1024]{1,0:T(8,128)(2,1)}, bf16[128,8192]{1,0:T(8,128)(2,1)}) custom-call(s32[1]{0:T(128)} %bitcast.refs_0_, bf16[128,2048]{1,0:T(8,128)(2,1)S(1)} %copy-done.12, f32[128,1024]{1,0:T(8,128)S(1)} %copy-done.14, f32[128,1024]{1,0:T(8,128)S(1)} %copy-done.16, bf16[128,3072]{1,0:T(8,128)(2,1)S(1)} %collective-permute-done.14.refs_4_, ...), custom_call_target="tpu_custom_call" | custom-call | flops 1 | bytes 1 | tf_op jit(solution)/shard_map/join_columns/pallas_call | solution.py:414
  (78 shorter events, 5.5 us)
Async XLA Ops:
  4.3 23.8 %all-to-all-start = ((bf16[16,8,1024]{2,1,0:T(8,128)(2,1)}), bf16[16,8,1024]{2,1,0:T(8,128)(2,1)S(1)}, u32[]{:S(2)}, u32[]{:S(2)}) async-start(bf16[16,8,1024]{2,1,0:T(8,128)(2,1)} %gather_fusion), calls=%async_computation | async-start | bytes 524288 | tf_op jit(solution)/shard_map/all_to_all | solution.py:457
  10.9 17.3 %collective-permute-start = (bf16[128,1024]{1,0:T(8,128)(2,1)S(1)}, bf16[128,1024]{1,0:T(8,128)(2,1)S(1)}, u32[]{:S(2)}, u32[]{:S(2)}) collective-permute-start(bf16[128,1024]{1,0:T(8,128)(2,1)S(1)} %mask_rows.1.refs_5_.refs_14_.refs_8_), channel_id=1, source_target_pairs={{0,8},{1,9},{2,10},{3,11},{4,12},{5,13},{6,14},{7,15},{8,0},{9,1},... | collective-permute-start | bytes 786440 | tf_op jit(solution)/shard_map/ppermute | solution.py:432
  13.0 16.7 %copy-start.19 = (s32[16]{0:T(128)S(1)}, s32[16]{0:T(128)}, u32[]{:S(2)}) copy-start(s32[16]{0:T(128)} %refs_0_) | copy-start | bytes 196
  13.0 16.7 %copy-start.20 = (s32[64]{0:T(128)S(1)}, s32[64]{0:T(128)}, u32[]{:S(2)}) copy-start(s32[64]{0:T(128)} %refs_2_.5) | copy-start | bytes 772
  16.7 58.2 %copy-start.3 = (bf16[8,512,128]{2,1,0:T(8,128)(2,1)S(1)}, bf16[8,512,128]{2,1,0:T(8,128)(2,1)}, u32[]{:S(2)}) copy-start(bf16[8,512,128]{2,1,0:T(8,128)(2,1)} %get-tuple-element.61.refs_1_.refs_6_) | copy-start | bytes 3145732
  28.2 24.2 %collective-permute-start.1 = (bf16[512,1024]{1,0:T(8,128)(2,1)}, bf16[512,1024]{1,0:T(8,128)(2,1)S(1)}, u32[]{:S(2)}, u32[]{:S(2)}) collective-permute-start(bf16[512,1024]{1,0:T(8,128)(2,1)} %refs_1_.6), channel_id=1, source_target_pairs={{0,2},{1,3},{2,0},{3,1},{4,6},{5,7},{6,4},{7,5},{8,10},{9,11},{10,... | collective-permute-start | bytes 3145736 | tf_op jit(solution)/shard_map/ppermute | solution.py:432
  28.4 46.5 %collective-permute-start.5 = (bf16[8,512,128]{2,1,0:T(8,128)(2,1)}, bf16[8,512,128]{2,1,0:T(8,128)(2,1)S(1)}, u32[]{:S(2)}, u32[]{:S(2)}) collective-permute-start(bf16[8,512,128]{2,1,0:T(8,128)(2,1)} %get-tuple-element.60), channel_id=1, source_target_pairs={{0,2},{1,3},{2,0},{3,1},{4,6},{5,7},{6,4},{7,5},{8,10},{9,11},{10,... | collective-permute-start | bytes 3145736 | tf_op jit(solution)/shard_map/ppermute | solution.py:432
  31.2 21.2 %copy-start.22 = (bf16[512,1024]{1,0:T(8,128)(2,1)S(1)}, bf16[512,1024]{1,0:T(8,128)(2,1)}, u32[]{:S(2)}) copy-start(bf16[512,1024]{1,0:T(8,128)(2,1)} %refs_1_.6) | copy-start | bytes 3145732
  32.1 53.7 %collective-permute-start.8 = (bf16[128,4224]{1,0:T(8,128)(2,1)S(1)}, bf16[128,4224]{1,0:T(8,128)(2,1)S(1)}, u32[]{:S(2)}, u32[]{:S(2)}) collective-permute-start(bf16[128,4224]{1,0:T(8,128)(2,1)S(1)} %get-tuple-element.64), channel_id=1, source_target_pairs={{0,4},{1,5},{2,6},{3,7},{4,0},{5,1},{6,2},{7,3},{8,12},{9,13},{10,... | collective-permute-start | bytes 3244040 | tf_op jit(solution)/shard_map/ppermute | solution.py:432
  35.1 41.5 %collective-permute-start.9 = (bf16[128,2176]{1,0:T(8,128)(2,1)S(1)}, bf16[128,2176]{1,0:T(8,128)(2,1)S(1)}, u32[]{:S(2)}, u32[]{:S(2)}) collective-permute-start(bf16[128,2176]{1,0:T(8,128)(2,1)S(1)} %get-tuple-element.65), channel_id=1, source_target_pairs={{0,8},{1,9},{2,10},{3,11},{4,12},{5,13},{6,14},{7,15},{8,0},{9,1},... | collective-permute-start | bytes 1671176 | tf_op jit(solution)/shard_map/ppermute | solution.py:432
  35.4 41.4 %collective-permute-start.10 = (bf16[128,2176]{1,0:T(8,128)(2,1)S(1)}, bf16[128,2176]{1,0:T(8,128)(2,1)S(1)}, u32[]{:S(2)}, u32[]{:S(2)}) collective-permute-start(bf16[128,2176]{1,0:T(8,128)(2,1)S(1)} %get-tuple-element.66), channel_id=1, source_target_pairs={{0,12},{1,13},{2,14},{3,15},{4,8},{5,9},{6,10},{7,11},{8,4},{9,5},... | collective-permute-start | bytes 1671176 | tf_op jit(solution)/shard_map/ppermute | solution.py:432
  52.4 24.3 %copy-start.21 = (bf16[512,1024]{1,0:T(8,128)(2,1)}, bf16[512,1024]{1,0:T(8,128)(2,1)S(1)}, u32[]{:S(2)}) copy-start(bf16[512,1024]{1,0:T(8,128)(2,1)S(1)} %collective-permute-done.1.refs_3_) | copy-start | bytes 3145732
  52.4 37.0 %collective-permute-start.2 = (bf16[512,1024]{1,0:T(8,128)(2,1)S(1)}, bf16[512,1024]{1,0:T(8,128)(2,1)}, u32[]{:S(2)}, u32[]{:S(2)}) collective-permute-start(bf16[512,1024]{1,0:T(8,128)(2,1)S(1)} %copy-done.22), channel_id=1, source_target_pairs={{0,1},{1,0},{2,3},{3,2},{4,5},{5,4},{6,7},{7,6},{8,9},{9,8},{10,11... | collective-permute-start | bytes 3145736 | tf_op jit(solution)/shard_map/ppermute | solution.py:432
  75.0 10.9 %collective-permute-start.7 = (bf16[4,512,128]{2,1,0:T(8,128)(2,1)S(1)}, bf16[4,512,128]{2,1,0:T(8,128)(2,1)S(1)}, u32[]{:S(2)}, u32[]{:S(2)}) collective-permute-start(bf16[4,512,128]{2,1,0:T(8,128)(2,1)S(1)} %slice.20), channel_id=1, source_target_pairs={{0,1},{1,0},{2,3},{3,2},{4,5},{5,4},{6,7},{7,6},{8,9},{9,8},{10,11... | collective-permute-start | bytes 1572872 | tf_op jit(solution)/shard_map/ppermute | solution.py:432
  76.6 9.3 %collective-permute-start.6 = (bf16[4,512,128]{2,1,0:T(8,128)(2,1)S(1)}, bf16[4,512,128]{2,1,0:T(8,128)(2,1)S(1)}, u32[]{:S(2)}, u32[]{:S(2)}) collective-permute-start(bf16[4,512,128]{2,1,0:T(8,128)(2,1)S(1)} %slice.14), channel_id=1, source_target_pairs={{0,1},{1,0},{2,3},{3,2},{4,5},{5,4},{6,7},{7,6},{8,9},{9,8},{10,11... | collective-permute-start | bytes 1572872 | tf_op jit(solution)/shard_map/ppermute | solution.py:432
  76.8 11.7 %collective-permute-start.4 = (bf16[256,1024]{1,0:T(8,128)(2,1)S(1)}, bf16[256,1024]{1,0:T(8,128)(2,1)S(1)}, u32[]{:S(2)}, u32[]{:S(2)}) collective-permute-start(bf16[256,1024]{1,0:T(8,128)(2,1)S(1)} %get-tuple-element.104), channel_id=1, source_target_pairs={{0,1},{1,0},{2,3},{3,2},{4,5},{5,4},{6,7},{7,6},{8,9},{9,8},{10,11... | collective-permute-start | bytes 1572872 | tf_op jit(solution)/shard_map/ppermute | solution.py:432
  85.8 3.6 %collective-permute-start.3 = (bf16[256,1024]{1,0:T(8,128)(2,1)S(1)}, bf16[256,1024]{1,0:T(8,128)(2,1)S(1)}, u32[]{:S(2)}, u32[]{:S(2)}) collective-permute-start(bf16[256,1024]{1,0:T(8,128)(2,1)S(1)} %get-tuple-element.105), channel_id=1, source_target_pairs={{0,1},{1,0},{2,3},{3,2},{4,5},{5,4},{6,7},{7,6},{8,9},{9,8},{10,11... | collective-permute-start | bytes 1572872 | tf_op jit(solution)/shard_map/ppermute | solution.py:432
  86.8 12.5 %collective-permute-start.11 = (f32[128,128]{1,0:T(8,128)S(1)}, f32[128,128]{1,0:T(8,128)S(1)}, u32[]{:S(2)}, u32[]{:S(2)}) collective-permute-start(f32[128,128]{1,0:T(8,128)S(1)} %get-tuple-element.68), channel_id=1, source_target_pairs={{0,4},{1,5},{2,6},{3,7},{4,0},{5,1},{6,2},{7,3},{8,12},{9,13},{10,... | collective-permute-start | bytes 196616 | tf_op jit(solution)/shard_map/ppermute | solution.py:432
  86.8 12.5 %collective-permute-start.12 = (f32[128,128]{1,0:T(8,128)S(1)}, f32[128,128]{1,0:T(8,128)S(1)}, u32[]{:S(2)}, u32[]{:S(2)}) collective-permute-start(f32[128,128]{1,0:T(8,128)S(1)} %get-tuple-element.69), channel_id=1, source_target_pairs={{0,8},{1,9},{2,10},{3,11},{4,12},{5,13},{6,14},{7,15},{8,0},{9,1},... | collective-permute-start | bytes 196616 | tf_op jit(solution)/shard_map/ppermute | solution.py:432
  88.4 10.8 %collective-permute-start.13 = (f32[128,128]{1,0:T(8,128)S(1)}, f32[128,128]{1,0:T(8,128)S(1)}, u32[]{:S(2)}, u32[]{:S(2)}) collective-permute-start(f32[128,128]{1,0:T(8,128)S(1)} %get-tuple-element.70), channel_id=1, source_target_pairs={{0,12},{1,13},{2,14},{3,15},{4,8},{5,9},{6,10},{7,11},{8,4},{9,5},... | collective-permute-start | bytes 196616 | tf_op jit(solution)/shard_map/ppermute | solution.py:432
  100.1 12.3 %copy-start.18 = (bf16[128,1024]{1,0:T(8,128)(2,1)}, bf16[128,1024]{1,0:T(8,128)(2,1)S(1)}, u32[]{:S(2)}) copy-start(bf16[128,1024]{1,0:T(8,128)(2,1)S(1)} %get-tuple-element.87) | copy-start | bytes 786436
  101.5 2.9 %collective-permute-start.17 = (bf16[512,640]{1,0:T(8,128)(2,1)S(1)}, bf16[512,640]{1,0:T(8,128)(2,1)S(1)}, u32[]{:S(2)}, u32[]{:S(2)}) collective-permute-start(bf16[512,640]{1,0:T(8,128)(2,1)S(1)} %get-tuple-element.93), channel_id=1, source_target_pairs={{0,1},{1,0},{2,3},{3,2},{4,5},{5,4},{6,7},{7,6},{8,9},{9,8},{10,11... | collective-permute-start | bytes 1966088 | tf_op jit(solution)/shard_map/ppermute | solution.py:432
  104.4 30.1 %collective-permute-start.18 = (bf16[512,640]{1,0:T(8,128)(2,1)}, bf16[512,640]{1,0:T(8,128)(2,1)}, u32[]{:S(2)}, u32[]{:S(2)}) collective-permute-start(bf16[512,640]{1,0:T(8,128)(2,1)} %get-tuple-element.96), channel_id=1, source_target_pairs={{0,2},{1,3},{2,0},{3,1},{4,6},{5,7},{6,4},{7,5},{8,10},{9,11},{10,... | collective-permute-start | bytes 1966088 | tf_op jit(solution)/shard_map/ppermute | solution.py:432
  104.7 7.3 %collective-permute-start.20 = (bf16[128,1024]{1,0:T(8,128)(2,1)S(1)}, bf16[128,1024]{1,0:T(8,128)(2,1)}, u32[]{:S(2)}, u32[]{:S(2)}) collective-permute-start(bf16[128,1024]{1,0:T(8,128)(2,1)S(1)} %get-tuple-element.81), channel_id=1, source_target_pairs={{0,4},{1,5},{2,6},{3,7},{4,0},{5,1},{6,2},{7,3},{8,12},{9,13},{10,... | collective-permute-start | bytes 786440 | tf_op jit(solution)/shard_map/ppermute | solution.py:432
  105.4 70.4 %collective-permute-start.14 = (bf16[128,3072]{1,0:T(8,128)(2,1)}, bf16[128,3072]{1,0:T(8,128)(2,1)S(1)}, u32[]{:S(2)}, u32[]{:S(2)}) collective-permute-start(bf16[128,3072]{1,0:T(8,128)(2,1)} %get-tuple-element.77), channel_id=1, source_target_pairs={{0,4},{1,5},{2,6},{3,7},{4,0},{5,1},{6,2},{7,3},{8,12},{9,13},{10,... | collective-permute-start | bytes 2359304 | tf_op jit(solution)/shard_map/ppermute | solution.py:432
  106.2 30.4 %collective-permute-start.19 = (bf16[512,640]{1,0:T(8,128)(2,1)}, bf16[512,640]{1,0:T(8,128)(2,1)}, u32[]{:S(2)}, u32[]{:S(2)}) collective-permute-start(bf16[512,640]{1,0:T(8,128)(2,1)} %get-tuple-element.97), channel_id=1, source_target_pairs={{0,3},{1,2},{2,1},{3,0},{4,7},{5,6},{6,5},{7,4},{8,11},{9,10},{10,... | collective-permute-start | bytes 1966088 | tf_op jit(solution)/shard_map/ppermute | solution.py:432
  108.5 67.3 %collective-permute-start.15 = (bf16[128,2048]{1,0:T(8,128)(2,1)}, bf16[128,2048]{1,0:T(8,128)(2,1)}, u32[]{:S(2)}, u32[]{:S(2)}) collective-permute-start(bf16[128,2048]{1,0:T(8,128)(2,1)} %get-tuple-element.78), channel_id=1, source_target_pairs={{0,8},{1,9},{2,10},{3,11},{4,12},{5,13},{6,14},{7,15},{8,0},{9,1},... | collective-permute-start | bytes 1572872 | tf_op jit(solution)/shard_map/ppermute | solution.py:432
  112.0 63.8 %collective-permute-start.16 = (bf16[128,2048]{1,0:T(8,128)(2,1)}, bf16[128,2048]{1,0:T(8,128)(2,1)}, u32[]{:S(2)}, u32[]{:S(2)}) collective-permute-start(bf16[128,2048]{1,0:T(8,128)(2,1)} %get-tuple-element.79), channel_id=1, source_target_pairs={{0,12},{1,13},{2,14},{3,15},{4,8},{5,9},{6,10},{7,11},{8,4},{9,5},... | collective-permute-start | bytes 1572872 | tf_op jit(solution)/shard_map/ppermute | solution.py:432
  112.4 60.4 %all-to-all-start.1 = ((bf16[16,8,1024]{2,1,0:T(8,128)(2,1)}), bf16[16,8,1024]{2,1,0:T(8,128)(2,1)S(1)}, u32[]{:S(2)}, u32[]{:S(2)}) async-start(bf16[16,8,1024]{2,1,0:T(8,128)(2,1)} %bitcast.5), calls=%async_computation.1 | async-start | bytes 524288 | tf_op jit(solution)/shard_map/all_to_all | solution.py:487
  134.5 41.3 %collective-permute-start.21 = (bf16[128,1024]{1,0:T(8,128)(2,1)}, bf16[128,1024]{1,0:T(8,128)(2,1)}, u32[]{:S(2)}, u32[]{:S(2)}) collective-permute-start(bf16[128,1024]{1,0:T(8,128)(2,1)} %add_convert_fusion), channel_id=1, source_target_pairs={{0,8},{1,9},{2,10},{3,11},{4,12},{5,13},{6,14},{7,15},{8,0},{9,1},... | collective-permute-start | bytes 786440 | tf_op jit(solution)/shard_map/ppermute | solution.py:432
  152.1 23.7 %copy-start.12 = (bf16[128,2048]{1,0:T(8,128)(2,1)S(1)}, bf16[128,2048]{1,0:T(8,128)(2,1)}, u32[]{:S(2)}) copy-start(bf16[128,2048]{1,0:T(8,128)(2,1)} %copy-done.11) | copy-start | bytes 1572868
  152.2 23.7 %copy-start.14 = (f32[128,1024]{1,0:T(8,128)S(1)}, f32[128,1024]{1,0:T(8,128)}, u32[]{:S(2)}) copy-start(f32[128,1024]{1,0:T(8,128)} %copy-done.13) | copy-start | bytes 1572868
  (15 other events, 99.1 us)

commit v4 on v3

--- a/solution.py
+++ b/solution.py
@@ -453,7 +453,7 @@
             evens = evens + [k ^ step for k in evens]
             step //= 2
 
-        up_send = jnp.take(expand_factor, after(block_adapter, masked), axis=0, mode="clip")
+        up_send = jnp.take(expand_factor, block_adapter, axis=0, mode="clip")
         up = lax.all_to_all(up_send, "fsdp", split_axis=0, concat_axis=0, tiled=True)
         up = up.reshape(rank, kv)
 

time: 182 us -> 180 us (0.989)
  waiting for transfers between devices: 72.2 us -> 70.1 us
where the time goes in v4:
time: 180 us; the launch traced here: 178 us
  waiting for transfers between devices  70.1 us (39%)
  starting transfers between devices  59.5 us (33%)
  Pallas kernels  39.2 us (22%)
  local copies, waits for them, and re-layouts  4.64 us (3%)
  other arithmetic  2.62 us (1%)
    ppermute x22, waiting for transfers between devices, swap(): return lax.ppermute(value, 'fsdp', [(i, i ^ mask) for i in range(devices)])  49.8 us
    ppermute x22, starting transfers between devices, swap(): return lax.ppermute(value, 'fsdp', [(i, i ^ mask) for i in range(devices)])  32.8 us
    all_to_all x1, waiting for transfers between devices, on_device(): lax.all_to_all(eg_got, 'fsdp', split_axis=0, concat_axis=0, tiled=True)  20.2 us
    all_to_all x1, starting transfers between devices, on_device(): lax.all_to_all(eg_got, 'fsdp', split_axis=0, concat_axis=0, tiled=True)  20.2 us
    pallas_call x1, Pallas kernels, down_grad(): pl.pallas_call(lambda *refs: down_kernel(per, blocks, rank, *refs), grid_...  15.9 us
    pallas_call x1, Pallas kernels, main_parts(): pl.pallas_call(lambda *refs: main_kernel(evens, outer, sub, kv, *refs), o...  9.79 us
    all_to_all x1, starting transfers between devices, on_device(): lax.all_to_all(up_send, 'fsdp', split_axis=0, concat_axis=0, tiled=True)  6.55 us
    pallas_call x1, Pallas kernels, pick(): pl.pallas_call(lambda *refs: pick_kernel(outer, *refs), out_shape=(picked...  3.74 us
  transfers between devices with their start and end apart: 24, of which 6 were waited for; matrix products, arithmetic and copies ran while one was open for 1% of the time, Pallas kernels for 19%

profile of v4, /device:TPU:11, one launch (start us, length us, event | category | flops | bytes accessed | tf_op | source)
XLA Modules:
  0.0 177.5 jit_solution(12317458266101072958)
XLA Ops:
  1.9 1.3 gather_fusion
  3.1 6.6 %all-to-all-start = ((bf16[16,8,1024]{2,1,0:T(8,128)(2,1)}), bf16[16,8,1024]{2,1,0:T(8,128)(2,1)S(1)}, u32[]{:S(2)}, u32[]{:S(2)}) async-start(bf16[16,8,1024]{2,1,0:T(8,128)(2,1)} %gather_fusion), calls=%async_computation | async-start | bytes 524288 | tf_op jit(solution)/shard_map/all_to_all | solution.py:457
  10.4 0.9 copy-done.17
  11.4 2.2 %collective-permute-start = (bf16[128,1024]{1,0:T(8,128)(2,1)S(1)}, bf16[128,1024]{1,0:T(8,128)(2,1)S(1)}, u32[]{:S(2)}, u32[]{:S(2)}) collective-permute-start(bf16[128,1024]{1,0:T(8,128)(2,1)S(1)} %mask_rows.1.refs_5_.refs_14_.refs_8_), channel_id=1, source_target_pairs={{0,8},{1,9},{2,10},{3,11},{4,12},{5,13},{6,14},{7,15},{8,0},{9,1},... | collective-permute-start | bytes 786440 | tf_op jit(solution)/shard_map/ppermute | solution.py:432
  13.5 3.7 %pick_factors.1 = (bf16[8,512,128]{2,1,0:T(8,128)(2,1)}, bf16[8,512,128]{2,1,0:T(8,128)(2,1)}) custom-call(s32[1]{0:T(128)} %bitcast.refs_0_, s32[16]{0:T(128)} %refs_0_, bf16[64,512,128]{2,1,0:T(8,128)(2,1)} %refs_2_.3), custom_call_target="tpu_custom_call" | custom-call | flops 1 | bytes 1 | tf_op jit(solution)/shard_map/pick_factors/pallas_call | solution.py:52
  17.3 9.7 %collective-permute-done.refs_6_.refs_15_ = bf16[128,1024]{1,0:T(8,128)(2,1)S(1)} collective-permute-done((bf16[128,1024]{1,0:T(8,128)(2,1)S(1)}, bf16[128,1024]{1,0:T(8,128)(2,1)S(1)}, u32[]{:S(2)}, u32[]{:S(2)}) %collective-permute-start) | collective-permute-done | bytes 262176 | tf_op jit(solution)/shard_map/ppermute | solution.py:432
  27.2 1.3 collective-permute-start.5
  28.5 1.6 copy-done.9
  30.1 0.9 first_sends.1
  30.9 3.0 %collective-permute-start.8 = (bf16[128,4224]{1,0:T(8,128)(2,1)S(1)}, bf16[128,4224]{1,0:T(8,128)(2,1)S(1)}, u32[]{:S(2)}, u32[]{:S(2)}) collective-permute-start(bf16[128,4224]{1,0:T(8,128)(2,1)S(1)} %get-tuple-element.62), channel_id=1, source_target_pairs={{0,4},{1,5},{2,6},{3,7},{4,0},{5,1},{6,2},{7,3},{8,12},{9,13},{10,... | collective-permute-start | bytes 3244040 | tf_op jit(solution)/shard_map/ppermute | solution.py:432
  34.2 1.0 collective-permute-start.10
  35.2 16.1 %collective-permute-done.1.refs_3_ = bf16[512,1024]{1,0:T(8,128)(2,1)S(1)} collective-permute-done((bf16[512,1024]{1,0:T(8,128)(2,1)}, bf16[512,1024]{1,0:T(8,128)(2,1)S(1)}, u32[]{:S(2)}, u32[]{:S(2)}) %collective-permute-start.1) | collective-permute-done | bytes 1048608 | tf_op jit(solution)/shard_map/ppermute | solution.py:432
  51.2 2.7 %collective-permute-start.2 = (bf16[512,1024]{1,0:T(8,128)(2,1)S(1)}, bf16[512,1024]{1,0:T(8,128)(2,1)}, u32[]{:S(2)}, u32[]{:S(2)}) collective-permute-start(bf16[512,1024]{1,0:T(8,128)(2,1)S(1)} %copy-done.22), channel_id=1, source_target_pairs={{0,1},{1,0},{2,3},{3,2},{4,5},{5,4},{6,7},{7,6},{8,9},{9,8},{10,11... | collective-permute-start | bytes 3145736 | tf_op jit(solution)/shard_map/ppermute | solution.py:432
  53.9 19.8 %collective-permute-done.5.refs_2_.refs_7_ = bf16[8,512,128]{2,1,0:T(8,128)(2,1)S(1)} collective-permute-done((bf16[8,512,128]{2,1,0:T(8,128)(2,1)}, bf16[8,512,128]{2,1,0:T(8,128)(2,1)S(1)}, u32[]{:S(2)}, u32[]{:S(2)}) %collective-permute-start.5) | collective-permute-done | bytes 1048608 | tf_op jit(solution)/shard_map/ppermute | solution.py:432
  73.8 1.6 collective-permute-start.7
  75.6 9.0 %collective-permute-start.4 = (bf16[256,1024]{1,0:T(8,128)(2,1)S(1)}, bf16[256,1024]{1,0:T(8,128)(2,1)S(1)}, u32[]{:S(2)}, u32[]{:S(2)}) collective-permute-start(bf16[256,1024]{1,0:T(8,128)(2,1)S(1)} %get-tuple-element.102), channel_id=1, source_target_pairs={{0,1},{1,0},{2,3},{3,2},{4,5},{5,4},{6,7},{7,6},{8,9},{9,8},{10,11... | collective-permute-start | bytes 1572872 | tf_op jit(solution)/shard_map/ppermute | solution.py:432
  85.6 1.7 collective-permute-start.12
  87.3 1.0 collective-permute-start.13
  88.3 9.8 %plane_products.1 = (bf16[128,2048]{1,0:T(8,128)(2,1)S(1)}, bf16[128,3072]{1,0:T(8,128)(2,1)}, bf16[128,2048]{1,0:T(8,128)(2,1)}, bf16[128,2048]{1,0:T(8,128)(2,...) custom-call(s32[1]{0:T(128)} %bitcast.refs_0_, bf16[512,1024]{1,0:T(8,128)(2,1)} %refs_1_.6, ...), custom_call_target="tpu_custom_call" | custom-call | flops 1 | bytes 1 | tf_op jit(solution)/shard_map/plane_products/pallas_call | solution.py:211
  99.0 1.3 pack_columns.1
  100.3 1.2 collective-permute-start.17
  101.5 1.7 collective-permute-done.17.refs_3_
  105.0 2.3 %collective-permute-start.19 = (bf16[512,640]{1,0:T(8,128)(2,1)}, bf16[512,640]{1,0:T(8,128)(2,1)}, u32[]{:S(2)}, u32[]{:S(2)}) collective-permute-start(bf16[512,640]{1,0:T(8,128)(2,1)} %get-tuple-element.95), channel_id=1, source_target_pairs={{0,3},{1,2},{2,1},{3,0},{4,7},{5,6},{6,5},{7,4},{8,11},{9,10},{10,... | collective-permute-start | bytes 1966088 | tf_op jit(solution)/shard_map/ppermute | solution.py:432
  107.3 1.1 collective-permute-start.15
  108.4 2.5 %collective-permute-done.20 = bf16[128,1024]{1,0:T(8,128)(2,1)} collective-permute-done((bf16[128,1024]{1,0:T(8,128)(2,1)S(1)}, bf16[128,1024]{1,0:T(8,128)(2,1)}, u32[]{:S(2)}, u32[]{:S(2)}) %collective-permute-start.20) | collective-permute-done | bytes 262176 | tf_op jit(solution)/shard_map/ppermute | solution.py:432
  111.3 20.2 %all-to-all-start.1 = ((bf16[16,8,1024]{2,1,0:T(8,128)(2,1)}), bf16[16,8,1024]{2,1,0:T(8,128)(2,1)S(1)}, u32[]{:S(2)}, u32[]{:S(2)}) async-start(bf16[16,8,1024]{2,1,0:T(8,128)(2,1)} %bitcast.5), calls=%async_computation.1 | async-start | bytes 524288 | tf_op jit(solution)/shard_map/all_to_all | solution.py:487
  131.4 1.9 %add_convert_fusion = bf16[128,1024]{1,0:T(8,128)(2,1)} fusion(f32[128,1024]{1,0:T(8,128)} %copy-done.10, bf16[128,1024]{1,0:T(8,128)(2,1)} %collective-permute-done.20), kind=kLoop, calls=%fused_computation.1 | loop fusion | flops 393216 | bytes 1048576 | tf_op jit(solution)/shard_map/convert_element_type | solution.py:498
  133.3 2.1 %collective-permute-start.21 = (bf16[128,1024]{1,0:T(8,128)(2,1)}, bf16[128,1024]{1,0:T(8,128)(2,1)}, u32[]{:S(2)}, u32[]{:S(2)}) collective-permute-start(bf16[128,1024]{1,0:T(8,128)(2,1)} %add_convert_fusion), channel_id=1, source_target_pairs={{0,8},{1,9},{2,10},{3,11},{4,12},{5,13},{6,14},{7,15},{8,0},{9,1},... | collective-permute-start | bytes 786440 | tf_op jit(solution)/shard_map/ppermute | solution.py:432
  135.4 15.9 %down_gradient.1 = f32[64,512,128]{2,1,0:T(8,128)} custom-call(s32[1]{0:T(128)} %bitcast.refs_0_, s32[16]{0:T(128)S(1)} %copy-done.19, bf16[512,640]{1,0:T(8,128)(2,1)S(1)} %get-tuple-element.90.refs_2_, bf16[512,640]{1,0:T(8,128)(2,1)S(1)} %collective-permute-done.17.refs_3_, bf16[512,640]{1,0:T(8,128)(2,1)} %collective-permute-done.18.refs_4_, ...), custom_call_target="tpu_custom_call" | custom-call | flops 1 | bytes 1 | tf_op jit(solution)/shard_map/down_gradient/pallas_call | solution.py:352
  151.4 20.2 %all-to-all-done.1.refs_1_ = bf16[16,8,1024]{2,1,0:T(8,128)(2,1)S(1)} async-done(((bf16[16,8,1024]{2,1,0:T(8,128)(2,1)}), bf16[16,8,1024]{2,1,0:T(8,128)(2,1)S(1)}, u32[]{:S(2)}, u32[]{:S(2)}) %all-to-all-start.1) | async-done | bytes 262176 | tf_op jit(solution)/shard_map/all_to_all | solution.py:487
  171.6 3.0 %up_gradient.1 = f32[64,8,1024]{2,1,0:T(8,128)} custom-call(s32[16]{0:T(128)S(1)} %copy-done.19, bf16[16,8,1024]{2,1,0:T(8,128)(2,1)S(1)} %all-to-all-done.1.refs_1_), custom_call_target="tpu_custom_call" | custom-call | flops 1 | bytes 1 | tf_op jit(solution)/shard_map/up_gradient/pallas_call | solution.py:386
  174.7 2.9 %join_columns.1 = (bf16[128,1024]{1,0:T(8,128)(2,1)}, bf16[128,8192]{1,0:T(8,128)(2,1)}) custom-call(s32[1]{0:T(128)} %bitcast.refs_0_, bf16[128,2048]{1,0:T(8,128)(2,1)S(1)} %copy-done.12, f32[128,1024]{1,0:T(8,128)S(1)} %copy-done.14, f32[128,1024]{1,0:T(8,128)S(1)} %copy-done.16, bf16[128,3072]{1,0:T(8,128)(2,1)S(1)} %collective-permute-done.14.refs_4_, ...), custom_call_target="tpu_custom_call" | custom-call | flops 1 | bytes 1 | tf_op jit(solution)/shard_map/join_columns/pallas_call | solution.py:414
  (78 shorter events, 6.1 us)
Async XLA Ops:
  3.1 23.8 %all-to-all-start = ((bf16[16,8,1024]{2,1,0:T(8,128)(2,1)}), bf16[16,8,1024]{2,1,0:T(8,128)(2,1)S(1)}, u32[]{:S(2)}, u32[]{:S(2)}) async-start(bf16[16,8,1024]{2,1,0:T(8,128)(2,1)} %gather_fusion), calls=%async_computation | async-start | bytes 524288 | tf_op jit(solution)/shard_map/all_to_all | solution.py:457
  11.4 15.6 %collective-permute-start = (bf16[128,1024]{1,0:T(8,128)(2,1)S(1)}, bf16[128,1024]{1,0:T(8,128)(2,1)S(1)}, u32[]{:S(2)}, u32[]{:S(2)}) collective-permute-start(bf16[128,1024]{1,0:T(8,128)(2,1)S(1)} %mask_rows.1.refs_5_.refs_14_.refs_8_), channel_id=1, source_target_pairs={{0,8},{1,9},{2,10},{3,11},{4,12},{5,13},{6,14},{7,15},{8,0},{9,1},... | collective-permute-start | bytes 786440 | tf_op jit(solution)/shard_map/ppermute | solution.py:432
  13.5 15.0 %copy-start.19 = (s32[16]{0:T(128)S(1)}, s32[16]{0:T(128)}, u32[]{:S(2)}) copy-start(s32[16]{0:T(128)} %refs_0_) | copy-start | bytes 196
  13.5 15.0 %copy-start.20 = (s32[64]{0:T(128)S(1)}, s32[64]{0:T(128)}, u32[]{:S(2)}) copy-start(s32[64]{0:T(128)} %refs_2_.5) | copy-start | bytes 772
  17.3 56.4 %copy-start.3 = (bf16[8,512,128]{2,1,0:T(8,128)(2,1)S(1)}, bf16[8,512,128]{2,1,0:T(8,128)(2,1)}, u32[]{:S(2)}) copy-start(bf16[8,512,128]{2,1,0:T(8,128)(2,1)} %get-tuple-element.59.refs_1_.refs_6_) | copy-start | bytes 3145732
  27.0 24.2 %collective-permute-start.1 = (bf16[512,1024]{1,0:T(8,128)(2,1)}, bf16[512,1024]{1,0:T(8,128)(2,1)S(1)}, u32[]{:S(2)}, u32[]{:S(2)}) collective-permute-start(bf16[512,1024]{1,0:T(8,128)(2,1)} %refs_1_.6), channel_id=1, source_target_pairs={{0,2},{1,3},{2,0},{3,1},{4,6},{5,7},{6,4},{7,5},{8,10},{9,11},{10,... | collective-permute-start | bytes 3145736 | tf_op jit(solution)/shard_map/ppermute | solution.py:432
  27.2 46.5 %collective-permute-start.5 = (bf16[8,512,128]{2,1,0:T(8,128)(2,1)}, bf16[8,512,128]{2,1,0:T(8,128)(2,1)S(1)}, u32[]{:S(2)}, u32[]{:S(2)}) collective-permute-start(bf16[8,512,128]{2,1,0:T(8,128)(2,1)} %get-tuple-element.58), channel_id=1, source_target_pairs={{0,2},{1,3},{2,0},{3,1},{4,6},{5,7},{6,4},{7,5},{8,10},{9,11},{10,... | collective-permute-start | bytes 3145736 | tf_op jit(solution)/shard_map/ppermute | solution.py:432
  30.1 21.2 %copy-start.22 = (bf16[512,1024]{1,0:T(8,128)(2,1)S(1)}, bf16[512,1024]{1,0:T(8,128)(2,1)}, u32[]{:S(2)}) copy-start(bf16[512,1024]{1,0:T(8,128)(2,1)} %refs_1_.6) | copy-start | bytes 3145732
  30.9 53.7 %collective-permute-start.8 = (bf16[128,4224]{1,0:T(8,128)(2,1)S(1)}, bf16[128,4224]{1,0:T(8,128)(2,1)S(1)}, u32[]{:S(2)}, u32[]{:S(2)}) collective-permute-start(bf16[128,4224]{1,0:T(8,128)(2,1)S(1)} %get-tuple-element.62), channel_id=1, source_target_pairs={{0,4},{1,5},{2,6},{3,7},{4,0},{5,1},{6,2},{7,3},{8,12},{9,13},{10,... | collective-permute-start | bytes 3244040 | tf_op jit(solution)/shard_map/ppermute | solution.py:432
  33.9 41.5 %collective-permute-start.9 = (bf16[128,2176]{1,0:T(8,128)(2,1)S(1)}, bf16[128,2176]{1,0:T(8,128)(2,1)S(1)}, u32[]{:S(2)}, u32[]{:S(2)}) collective-permute-start(bf16[128,2176]{1,0:T(8,128)(2,1)S(1)} %get-tuple-element.63), channel_id=1, source_target_pairs={{0,8},{1,9},{2,10},{3,11},{4,12},{5,13},{6,14},{7,15},{8,0},{9,1},... | collective-permute-start | bytes 1671176 | tf_op jit(solution)/shard_map/ppermute | solution.py:432
  34.2 41.4 %collective-permute-start.10 = (bf16[128,2176]{1,0:T(8,128)(2,1)S(1)}, bf16[128,2176]{1,0:T(8,128)(2,1)S(1)}, u32[]{:S(2)}, u32[]{:S(2)}) collective-permute-start(bf16[128,2176]{1,0:T(8,128)(2,1)S(1)} %get-tuple-element.64), channel_id=1, source_target_pairs={{0,12},{1,13},{2,14},{3,15},{4,8},{5,9},{6,10},{7,11},{8,4},{9,5},... | collective-permute-start | bytes 1671176 | tf_op jit(solution)/shard_map/ppermute | solution.py:432
  51.2 24.3 %copy-start.21 = (bf16[512,1024]{1,0:T(8,128)(2,1)}, bf16[512,1024]{1,0:T(8,128)(2,1)S(1)}, u32[]{:S(2)}) copy-start(bf16[512,1024]{1,0:T(8,128)(2,1)S(1)} %collective-permute-done.1.refs_3_) | copy-start | bytes 3145732
  51.2 37.0 %collective-permute-start.2 = (bf16[512,1024]{1,0:T(8,128)(2,1)S(1)}, bf16[512,1024]{1,0:T(8,128)(2,1)}, u32[]{:S(2)}, u32[]{:S(2)}) collective-permute-start(bf16[512,1024]{1,0:T(8,128)(2,1)S(1)} %copy-done.22), channel_id=1, source_target_pairs={{0,1},{1,0},{2,3},{3,2},{4,5},{5,4},{6,7},{7,6},{8,9},{9,8},{10,11... | collective-permute-start | bytes 3145736 | tf_op jit(solution)/shard_map/ppermute | solution.py:432
  73.8 10.9 %collective-permute-start.7 = (bf16[4,512,128]{2,1,0:T(8,128)(2,1)S(1)}, bf16[4,512,128]{2,1,0:T(8,128)(2,1)S(1)}, u32[]{:S(2)}, u32[]{:S(2)}) collective-permute-start(bf16[4,512,128]{2,1,0:T(8,128)(2,1)S(1)} %slice.20), channel_id=1, source_target_pairs={{0,1},{1,0},{2,3},{3,2},{4,5},{5,4},{6,7},{7,6},{8,9},{9,8},{10,11... | collective-permute-start | bytes 1572872 | tf_op jit(solution)/shard_map/ppermute | solution.py:432
  75.4 9.3 %collective-permute-start.6 = (bf16[4,512,128]{2,1,0:T(8,128)(2,1)S(1)}, bf16[4,512,128]{2,1,0:T(8,128)(2,1)S(1)}, u32[]{:S(2)}, u32[]{:S(2)}) collective-permute-start(bf16[4,512,128]{2,1,0:T(8,128)(2,1)S(1)} %slice.14), channel_id=1, source_target_pairs={{0,1},{1,0},{2,3},{3,2},{4,5},{5,4},{6,7},{7,6},{8,9},{9,8},{10,11... | collective-permute-start | bytes 1572872 | tf_op jit(solution)/shard_map/ppermute | solution.py:432
  75.6 11.7 %collective-permute-start.4 = (bf16[256,1024]{1,0:T(8,128)(2,1)S(1)}, bf16[256,1024]{1,0:T(8,128)(2,1)S(1)}, u32[]{:S(2)}, u32[]{:S(2)}) collective-permute-start(bf16[256,1024]{1,0:T(8,128)(2,1)S(1)} %get-tuple-element.102), channel_id=1, source_target_pairs={{0,1},{1,0},{2,3},{3,2},{4,5},{5,4},{6,7},{7,6},{8,9},{9,8},{10,11... | collective-permute-start | bytes 1572872 | tf_op jit(solution)/shard_map/ppermute | solution.py:432
  84.6 3.6 %collective-permute-start.3 = (bf16[256,1024]{1,0:T(8,128)(2,1)S(1)}, bf16[256,1024]{1,0:T(8,128)(2,1)S(1)}, u32[]{:S(2)}, u32[]{:S(2)}) collective-permute-start(bf16[256,1024]{1,0:T(8,128)(2,1)S(1)} %get-tuple-element.103), channel_id=1, source_target_pairs={{0,1},{1,0},{2,3},{3,2},{4,5},{5,4},{6,7},{7,6},{8,9},{9,8},{10,11... | collective-permute-start | bytes 1572872 | tf_op jit(solution)/shard_map/ppermute | solution.py:432
  85.6 12.5 %collective-permute-start.11 = (f32[128,128]{1,0:T(8,128)S(1)}, f32[128,128]{1,0:T(8,128)S(1)}, u32[]{:S(2)}, u32[]{:S(2)}) collective-permute-start(f32[128,128]{1,0:T(8,128)S(1)} %get-tuple-element.66), channel_id=1, source_target_pairs={{0,4},{1,5},{2,6},{3,7},{4,0},{5,1},{6,2},{7,3},{8,12},{9,13},{10,... | collective-permute-start | bytes 196616 | tf_op jit(solution)/shard_map/ppermute | solution.py:432
  85.6 12.5 %collective-permute-start.12 = (f32[128,128]{1,0:T(8,128)S(1)}, f32[128,128]{1,0:T(8,128)S(1)}, u32[]{:S(2)}, u32[]{:S(2)}) collective-permute-start(f32[128,128]{1,0:T(8,128)S(1)} %get-tuple-element.67), channel_id=1, source_target_pairs={{0,8},{1,9},{2,10},{3,11},{4,12},{5,13},{6,14},{7,15},{8,0},{9,1},... | collective-permute-start | bytes 196616 | tf_op jit(solution)/shard_map/ppermute | solution.py:432
  87.3 10.8 %collective-permute-start.13 = (f32[128,128]{1,0:T(8,128)S(1)}, f32[128,128]{1,0:T(8,128)S(1)}, u32[]{:S(2)}, u32[]{:S(2)}) collective-permute-start(f32[128,128]{1,0:T(8,128)S(1)} %get-tuple-element.68), channel_id=1, source_target_pairs={{0,12},{1,13},{2,14},{3,15},{4,8},{5,9},{6,10},{7,11},{8,4},{9,5},... | collective-permute-start | bytes 196616 | tf_op jit(solution)/shard_map/ppermute | solution.py:432
  98.9 12.3 %copy-start.18 = (bf16[128,1024]{1,0:T(8,128)(2,1)}, bf16[128,1024]{1,0:T(8,128)(2,1)S(1)}, u32[]{:S(2)}) copy-start(bf16[128,1024]{1,0:T(8,128)(2,1)S(1)} %get-tuple-element.85) | copy-start | bytes 786436
  100.3 2.9 %collective-permute-start.17 = (bf16[512,640]{1,0:T(8,128)(2,1)S(1)}, bf16[512,640]{1,0:T(8,128)(2,1)S(1)}, u32[]{:S(2)}, u32[]{:S(2)}) collective-permute-start(bf16[512,640]{1,0:T(8,128)(2,1)S(1)} %get-tuple-element.91), channel_id=1, source_target_pairs={{0,1},{1,0},{2,3},{3,2},{4,5},{5,4},{6,7},{7,6},{8,9},{9,8},{10,11... | collective-permute-start | bytes 1966088 | tf_op jit(solution)/shard_map/ppermute | solution.py:432
  103.3 30.0 %collective-permute-start.18 = (bf16[512,640]{1,0:T(8,128)(2,1)}, bf16[512,640]{1,0:T(8,128)(2,1)}, u32[]{:S(2)}, u32[]{:S(2)}) collective-permute-start(bf16[512,640]{1,0:T(8,128)(2,1)} %get-tuple-element.94), channel_id=1, source_target_pairs={{0,2},{1,3},{2,0},{3,1},{4,6},{5,7},{6,4},{7,5},{8,10},{9,11},{10,... | collective-permute-start | bytes 1966088 | tf_op jit(solution)/shard_map/ppermute | solution.py:432
  103.6 7.3 %collective-permute-start.20 = (bf16[128,1024]{1,0:T(8,128)(2,1)S(1)}, bf16[128,1024]{1,0:T(8,128)(2,1)}, u32[]{:S(2)}, u32[]{:S(2)}) collective-permute-start(bf16[128,1024]{1,0:T(8,128)(2,1)S(1)} %get-tuple-element.79), channel_id=1, source_target_pairs={{0,4},{1,5},{2,6},{3,7},{4,0},{5,1},{6,2},{7,3},{8,12},{9,13},{10,... | collective-permute-start | bytes 786440 | tf_op jit(solution)/shard_map/ppermute | solution.py:432
  104.3 70.4 %collective-permute-start.14 = (bf16[128,3072]{1,0:T(8,128)(2,1)}, bf16[128,3072]{1,0:T(8,128)(2,1)S(1)}, u32[]{:S(2)}, u32[]{:S(2)}) collective-permute-start(bf16[128,3072]{1,0:T(8,128)(2,1)} %get-tuple-element.75), channel_id=1, source_target_pairs={{0,4},{1,5},{2,6},{3,7},{4,0},{5,1},{6,2},{7,3},{8,12},{9,13},{10,... | collective-permute-start | bytes 2359304 | tf_op jit(solution)/shard_map/ppermute | solution.py:432
  105.0 30.4 %collective-permute-start.19 = (bf16[512,640]{1,0:T(8,128)(2,1)}, bf16[512,640]{1,0:T(8,128)(2,1)}, u32[]{:S(2)}, u32[]{:S(2)}) collective-permute-start(bf16[512,640]{1,0:T(8,128)(2,1)} %get-tuple-element.95), channel_id=1, source_target_pairs={{0,3},{1,2},{2,1},{3,0},{4,7},{5,6},{6,5},{7,4},{8,11},{9,10},{10,... | collective-permute-start | bytes 1966088 | tf_op jit(solution)/shard_map/ppermute | solution.py:432
  107.3 67.3 %collective-permute-start.15 = (bf16[128,2048]{1,0:T(8,128)(2,1)}, bf16[128,2048]{1,0:T(8,128)(2,1)}, u32[]{:S(2)}, u32[]{:S(2)}) collective-permute-start(bf16[128,2048]{1,0:T(8,128)(2,1)} %get-tuple-element.76), channel_id=1, source_target_pairs={{0,8},{1,9},{2,10},{3,11},{4,12},{5,13},{6,14},{7,15},{8,0},{9,1},... | collective-permute-start | bytes 1572872 | tf_op jit(solution)/shard_map/ppermute | solution.py:432
  110.9 63.8 %collective-permute-start.16 = (bf16[128,2048]{1,0:T(8,128)(2,1)}, bf16[128,2048]{1,0:T(8,128)(2,1)}, u32[]{:S(2)}, u32[]{:S(2)}) collective-permute-start(bf16[128,2048]{1,0:T(8,128)(2,1)} %get-tuple-element.77), channel_id=1, source_target_pairs={{0,12},{1,13},{2,14},{3,15},{4,8},{5,9},{6,10},{7,11},{8,4},{9,5},... | collective-permute-start | bytes 1572872 | tf_op jit(solution)/shard_map/ppermute | solution.py:432
  111.3 60.3 %all-to-all-start.1 = ((bf16[16,8,1024]{2,1,0:T(8,128)(2,1)}), bf16[16,8,1024]{2,1,0:T(8,128)(2,1)S(1)}, u32[]{:S(2)}, u32[]{:S(2)}) async-start(bf16[16,8,1024]{2,1,0:T(8,128)(2,1)} %bitcast.5), calls=%async_computation.1 | async-start | bytes 524288 | tf_op jit(solution)/shard_map/all_to_all | solution.py:487
  133.3 41.3 %collective-permute-start.21 = (bf16[128,1024]{1,0:T(8,128)(2,1)}, bf16[128,1024]{1,0:T(8,128)(2,1)}, u32[]{:S(2)}, u32[]{:S(2)}) collective-permute-start(bf16[128,1024]{1,0:T(8,128)(2,1)} %add_convert_fusion), channel_id=1, source_target_pairs={{0,8},{1,9},{2,10},{3,11},{4,12},{5,13},{6,14},{7,15},{8,0},{9,1},... | collective-permute-start | bytes 786440 | tf_op jit(solution)/shard_map/ppermute | solution.py:432
  151.4 23.3 %copy-start.12 = (bf16[128,2048]{1,0:T(8,128)(2,1)S(1)}, bf16[128,2048]{1,0:T(8,128)(2,1)}, u32[]{:S(2)}) copy-start(bf16[128,2048]{1,0:T(8,128)(2,1)} %copy-done.11) | copy-start | bytes 1572868
  151.4 23.3 %copy-start.14 = (f32[128,1024]{1,0:T(8,128)S(1)}, f32[128,1024]{1,0:T(8,128)}, u32[]{:S(2)}) copy-start(f32[128,1024]{1,0:T(8,128)} %copy-done.13) | copy-start | bytes 1572868
  (15 other events, 97.9 us)
